TPU v7x, 512 devices: a whole 4x8x8 slice. The times are simulated.
512 devices in a mesh: graph: 16 (over z, core), config: 32 (over y, x).
Axes of the slice: x: 4, y: 8, z: 8, core: 2. Of those that a mesh axis runs over, the one named last changes fastest.
Arguments:
- features: bfloat16 [64, 8192, 128], P('config', 'graph'), may hold values from -6 to 6
- cotangent: bfloat16 [64, 8192, 128], P(None, ('graph', 'config')), may hold values from -6 to 6
- sage_weight: bfloat16 [2, 128, 128], replicated, may hold values from -0.5 to 0.5
- attn_weight: bfloat16 [4, 128, 128], replicated, may hold values from -0.5 to 0.5
- tile_vals: bfloat16 [192, 128, 128], P('graph'), may hold values from -0.375 to 0.375
- tile_dst: int32 [192], P('graph'), may hold values from 0 to 3
- tile_src: int32 [192], P('graph'), may hold values from 0 to 3
- tile_count: int32 [16], P('graph'), may hold values from 3 to 12, as said below
- hub_ids: int32 [128], P('graph'), may hold values from 0 to 8191, as said below
- hub_weight: bfloat16 [8192, 128], P('graph'), may hold values from -0.5 to 0.5
Outputs:
- layer_out: bfloat16 [64, 8192, 128], P(None, ('graph', 'config'))
- grad_features: bfloat16 [64, 8192, 128], P('config', 'graph')
- grad_weights: float32 [16, 6, 128, 128], P('graph')
Inputs may be any that keep to these rules, and one draw needn't show every extreme that they name: Slot t of slab g (t counted within the slab) is live when t < tile_count[g]; some slab has all 12 slots live. `hub_ids`: entries g * 8 to (g+1) * 8 - 1 are distinct nodes of slab g.
All inputs are finite; a program needn't handle non-finite values.
Results may differ from a plain program's by a relative error of at most 0.024.
Values may be sent and summed in bfloat16 or wider, within the bound.
A program may use at most 64 MiB of HBM per device.

v0:
```python
import math

import jax
import jax.numpy as jnp
from jax import lax
from jax.sharding import PartitionSpec as P

HEADS = 4


CAP = 20.0


def attend(queries, key_rows, value_rows):
    layout_count, node_count, feature_width = queries.shape
    head_size = feature_width // HEADS
    split = (layout_count, node_count, HEADS, head_size)
    query_b = queries.reshape(split)
    key_b = key_rows.reshape(split)
    value_b = value_rows.reshape(split)
    scores = jnp.einsum(
        "lkhd,mkhd->khlm", query_b, key_b, preferred_element_type=jnp.float32
    ) / math.sqrt(head_size)
    capped = CAP * jnp.tanh(scores / CAP)
    weights = jnp.exp(capped)
    attention = weights / jnp.sum(weights, axis=-1, keepdims=True)
    attention = attention.astype(value_b.dtype)
    mixture = jnp.einsum("khlm,mkhd->lkhd", attention, value_b, preferred_element_type=jnp.float32)
    return mixture.reshape(layout_count, node_count, feature_width).astype(queries.dtype)


def project(flat_rows, weight):
    return jnp.dot(flat_rows, weight, preferred_element_type=jnp.float32)


def project_back(flat_rows, weight):
    return jnp.dot(flat_rows, weight.T, preferred_element_type=jnp.float32)


def outer_sum(left_rows, right_rows):
    return jnp.dot(left_rows.T, right_rows, preferred_element_type=jnp.float32)


def sage_forward(feats, aggregate, sage_weight):
    shaped = feats.shape
    width_f = shaped[-1]
    pre_acts = project(feats.reshape(-1, width_f), sage_weight[0]) + project(
        aggregate.reshape(-1, width_f), sage_weight[1]
    )
    hidden = jax.nn.silu(pre_acts).astype(jnp.bfloat16)
    return (pre_acts.reshape(shaped), hidden.reshape(shaped))


def node_forward(hidden, attn_weight):
    shaped = hidden.shape
    width_f = shaped[-1]
    three = (shaped[0], -1, width_f)
    flat_hidden = hidden.reshape(-1, width_f)
    queries = project(flat_hidden, attn_weight[0]).astype(jnp.bfloat16)
    key_rows = project(flat_hidden, attn_weight[1]).astype(jnp.bfloat16)
    value_rows = project(flat_hidden, attn_weight[2]).astype(jnp.bfloat16)
    mixture = attend(queries.reshape(three), key_rows.reshape(three), value_rows.reshape(three))
    output = (
        flat_hidden.astype(jnp.float32) + project(mixture.reshape(-1, width_f), attn_weight[3])
    ).astype(jnp.bfloat16)
    return (
        output.reshape(shaped),
        queries.reshape(shaped),
        key_rows.reshape(shaped),
        value_rows.reshape(shaped),
        mixture.reshape(shaped),
    )


def node_backward(cot_rows, hidden, queries, key_rows, value_rows, mixture, attn_weight):
    shaped = hidden.shape
    width_f = shaped[-1]
    three = (shaped[0], -1, width_f)
    flat_cot = cot_rows.reshape(-1, width_f)
    grad_mix = project_back(flat_cot, attn_weight[3]).astype(jnp.bfloat16)
    grad_wo = outer_sum(mixture.reshape(-1, width_f), flat_cot)
    unused, pullback = jax.vjp(attend, queries, key_rows, value_rows)
    grad_q, grad_k, grad_v = pullback(grad_mix.reshape(three))
    flat_q = grad_q.reshape(-1, width_f)
    flat_k = grad_k.reshape(-1, width_f)
    flat_v = grad_v.reshape(-1, width_f)
    grad_hidden = (
        flat_cot.astype(jnp.float32)
        + project_back(flat_q, attn_weight[0])
        + project_back(flat_k, attn_weight[1])
        + project_back(flat_v, attn_weight[2])
    ).astype(jnp.bfloat16)
    flat_hidden = hidden.reshape(-1, width_f)
    grads = jnp.stack(
        [
            outer_sum(flat_hidden, flat_q),
            outer_sum(flat_hidden, flat_k),
            outer_sum(flat_hidden, flat_v),
            grad_wo,
        ]
    )
    return (grad_hidden.reshape(shaped), grads)


def sage_backward(grad_hidden, pre_acts, feats, aggregate, sage_weight):
    shaped = feats.shape
    width_f = shaped[-1]
    flat_pre = pre_acts.reshape(-1, width_f)
    sigmoid_pre = jax.nn.sigmoid(flat_pre)
    grad_pre = (
        grad_hidden.reshape(-1, width_f).astype(jnp.float32)
        * sigmoid_pre
        * (1.0 + flat_pre * (1.0 - sigmoid_pre))
    ).astype(jnp.bfloat16)
    grads = jnp.stack(
        [
            outer_sum(feats.reshape(-1, width_f), grad_pre),
            outer_sum(aggregate.reshape(-1, width_f), grad_pre),
        ]
    )
    grad_self = project_back(grad_pre, sage_weight[0]).astype(jnp.bfloat16).reshape(shaped)
    grad_agg = project_back(grad_pre, sage_weight[1]).astype(jnp.bfloat16).reshape(shaped)
    return (grad_self, grad_agg, grads)


def tile_forward(source, tile_vals, tile_src, tile_dst, live):
    layout_count, node_count, width_f = source.shape
    tile_size = tile_vals.shape[1]
    block_count = node_count // tile_size
    blocks = source.reshape(layout_count, block_count, tile_size, width_f)[:, tile_src]
    products = jnp.einsum("tij,ltjf->tlif", tile_vals, blocks, preferred_element_type=jnp.float32)
    products = products * live[:, None, None, None]
    summed = jax.ops.segment_sum(products, tile_dst, num_segments=block_count)
    return summed.transpose(1, 0, 2, 3).reshape(layout_count, node_count, width_f)


def tile_backward(grad_agg, tile_vals, tile_dst, tile_src, live):
    layout_count, node_count, width_f = grad_agg.shape
    tile_size = tile_vals.shape[1]
    block_count = node_count // tile_size
    blocks = grad_agg.reshape(layout_count, block_count, tile_size, width_f)[:, tile_dst]
    products = jnp.einsum("tij,ltif->tljf", tile_vals, blocks, preferred_element_type=jnp.float32)
    products = products * live[:, None, None, None]
    summed = jax.ops.segment_sum(products, tile_src, num_segments=block_count)
    return summed.transpose(1, 0, 2, 3).reshape(layout_count, node_count, width_f)


def flatten_nodes(arrays):
    return tuple((item.reshape(item.shape[0], -1, item.shape[-1]) for item in arrays))


def local(
    features,
    cotangent,
    sage_weight,
    attn_weight,
    tile_vals,
    tile_dst,
    tile_src,
    tile_count,
    hub_ids,
    hub_weight,
):
    layout_dev, node_dev, width_f = features.shape
    config_count = lax.axis_size("config")
    node_share = node_dev // config_count
    slab_index = lax.axis_index("graph")
    hub_local = hub_ids - slab_index * node_dev
    live = (jnp.arange(tile_dst.shape[0], dtype=jnp.int32) < tile_count[0]).astype(jnp.float32)
    local_hubs = features[:, hub_local]
    columns = hub_weight
    hub_sum = jnp.einsum(
        "nj,ljf->lnf",
        columns,
        lax.all_gather(local_hubs, "graph", axis=1, tiled=True),
        preferred_element_type=jnp.float32,
    )
    aggregate = (tile_forward(features, tile_vals, tile_src, tile_dst, live) + hub_sum).astype(
        jnp.bfloat16
    )
    split_shape = (layout_dev, config_count, node_share, width_f)
    back_shape = (layout_dev * config_count, 1, node_share, width_f)
    received = (
        lax.all_to_all(
            features.reshape(split_shape), "config", split_axis=1, concat_axis=0, tiled=True
        ),
        lax.all_to_all(
            aggregate.reshape(split_shape), "config", split_axis=1, concat_axis=0, tiled=True
        ),
    )
    pre_in, hidden_in = sage_forward(received[0], received[1], sage_weight)
    results = (received[0], received[1], pre_in, hidden_in) + node_forward(hidden_in, attn_weight)
    feats_node, agg_node, pre_node, hidden_node, output, queries, key_rows, value_rows, mixture = (
        flatten_nodes(results)
    )
    grad_hidden, attn_grads = node_backward(
        cotangent, hidden_node, queries, key_rows, value_rows, mixture, attn_weight
    )
    self_node, aggr_node, sage_grads = sage_backward(
        grad_hidden, pre_node, feats_node, agg_node, sage_weight
    )
    self_back, agg_back = (
        lax.all_to_all(
            self_node.reshape(back_shape), "config", split_axis=0, concat_axis=1, tiled=True
        ),
        lax.all_to_all(
            aggr_node.reshape(back_shape), "config", split_axis=0, concat_axis=1, tiled=True
        ),
    )
    grad_self = self_back.reshape(layout_dev, node_dev, width_f)
    grad_agg = agg_back.reshape(layout_dev, node_dev, width_f)
    back_rows = tile_backward(grad_agg, tile_vals, tile_dst, tile_src, live)
    columns = hub_weight
    hub_grads = lax.psum_scatter(
        jnp.einsum("nj,lnf->jlf", columns, grad_agg, preferred_element_type=jnp.float32).astype(
            jnp.bfloat16
        ),
        "graph",
        scatter_dimension=0,
        tiled=True,
    ).astype(jnp.float32)
    totals = grad_self.astype(jnp.float32) + back_rows
    totals = totals.at[:, hub_local].add(jnp.transpose(hub_grads, (1, 0, 2)))
    grad_features = totals.astype(jnp.bfloat16)
    partial_grads = jnp.concatenate([sage_grads, attn_grads], axis=0)
    summed = lax.psum(partial_grads.astype(jnp.bfloat16), "config").astype(jnp.float32)
    scale = 1.0 / math.sqrt(layout_dev * config_count * node_dev)
    return (output, grad_features, (summed * scale)[None])


def solution(mesh):
    return jax.shard_map(
        local,
        mesh=mesh,
        in_specs=(
            P("config", "graph", None),
            P(None, ("graph", "config"), None),
            P(),
            P(),
            P("graph", None, None),
            P("graph"),
            P("graph"),
            P("graph"),
            P("graph"),
            P("graph", None),
        ),
        out_specs=(
            P(None, ("graph", "config"), None),
            P("config", "graph", None),
            P("graph", None, None, None),
        ),
        check_vma=False,
    )
```

profile of v0, /device:TPU:1, one launch (start us, length us, event | category | flops | bytes accessed | tf_op | source)
XLA Modules:
  0.0 400.2 jit_solution(9092489679401032103)
XLA Ops:
  8.0 1.7 copy.116
  9.7 10.5 %all-to-all-start = ((bf16[2,32,16,128]{3,2,0,1:T(8,128)(2,1)}), bf16[2,32,16,128]{3,2,0,1:T(8,128)(2,1)S(1)}, u32[]{:S(2)}, u32[]{:S(2)}) async-start(bf16[2,32,16,128]{3,2,0,1:T(8,128)(2,1)} %copy.116), calls=%async_computation | async-start | bytes 524288 | tf_op jit(solution)/shard_map/all_to_all | solution.py:184
  24.4 1.6 gather_fusion
  27.7 1.9 copy.118
  29.6 1.8 scatter_fusion
  32.0 24.1 %all-gather = bf16[2,128,128]{2,1,0:T(8,128)(2,1)S(1)} all-gather(bf16[2,8,128]{2,1,0:T(8,128)(2,1)S(1)} %bitcast.206), channel_id=2, replica_groups=mesh['graph'=16,'config'=32] {'graph'}, dimensions={1}, use_global_device_ids=true | all-gather | bytes 69632 | tf_op jit(solution)/shard_map/all_gather | solution.py:175
  57.2 9.8 %all-to-all-start.1 = ((bf16[2,32,16,128]{3,2,0,1:T(8,128)(2,1)}), bf16[2,32,16,128]{3,2,0,1:T(8,128)(2,1)S(1)}, u32[]{:S(2)}, u32[]{:S(2)}) async-start(bf16[2,32,16,128]{3,2,0,1:T(8,128)(2,1)} %copy.121), calls=%async_computation.1 | async-start | bytes 524288 | tf_op jit(solution)/shard_map/all_to_all | solution.py:187
  71.1 7.6 %all-to-all-done.1 = bf16[2,32,16,128]{3,2,0,1:T(8,128)(2,1)S(1)} async-done(((bf16[2,32,16,128]{3,2,0,1:T(8,128)(2,1)}), bf16[2,32,16,128]{3,2,0,1:T(8,128)(2,1)S(1)}, u32[]{:S(2)}, u32[]{:S(2)}) %all-to-all-start.1) | async-done | bytes 262176 | tf_op jit(solution)/shard_map/all_to_all | solution.py:187
  82.7 2.1 reshape_reshape.25
  84.8 1.8 copy.123
  86.6 3.2 fusion.7
  91.5 1.9 copy.124
  93.4 2.8 fusion.6
  101.8 1.6 copy.134
  104.0 2.5 copy.131
  108.1 2.5 copy.137
  117.0 4.4 %all-to-all-start.3 = ((bf16[64,1,16,128]{3,2,1,0:T(8,128)(2,1)}), bf16[64,1,16,128]{3,2,1,0:T(8,128)(2,1)S(1)}, u32[]{:S(2)}, u32[]{:S(2)}) async-start(bf16[64,1,16,128]{3,2,1,0:T(8,128)(2,1)} %bitcast.37), calls=%async_computation.3 | async-start | bytes 524288 | tf_op jit(solution)/shard_map/all_to_all | solution.py:206
  124.7 1.7 fusion.13
  127.3 4.5 %all-to-all-done.3 = bf16[64,1,16,128]{3,2,1,0:T(8,128)(2,1)S(1)} async-done(((bf16[64,1,16,128]{3,2,1,0:T(8,128)(2,1)}), bf16[64,1,16,128]{3,2,1,0:T(8,128)(2,1)S(1)}, u32[]{:S(2)}, u32[]{:S(2)}) %all-to-all-start.3) | async-done | bytes 262176 | tf_op jit(solution)/shard_map/all_to_all | solution.py:206
  131.8 5.2 %all-to-all-start.2 = ((bf16[64,1,16,128]{3,2,1,0:T(8,128)(2,1)}), bf16[64,1,16,128]{3,2,1,0:T(8,128)(2,1)S(1)}, u32[]{:S(2)}, u32[]{:S(2)}) async-start(bf16[64,1,16,128]{3,2,1,0:T(8,128)(2,1)} %bitcast.32), calls=%async_computation.2 | async-start | bytes 524288 | tf_op jit(solution)/shard_map/all_to_all | solution.py:203
  137.1 136.1 %all-reduce.4.cloned.1.call-done = bf16[6,128,128]{1,2,0:T(8,128)(2,1)} async-done(((bf16[6,128,128]{1,2,0:T(8,128)(2,1)}), bf16[6,128,128]{1,2,0:T(8,128)(2,1)}) %all-reduce.4.cloned.1.call-update) | async-done | bytes 196624 | tf_op jit(solution)/shard_map/psum | solution.py:226
  277.3 1.9 copy.143
  279.3 1.8 scatter_fusion.1
  283.9 106.4 %all-reduce.6.cloned.1.call-done = bf16[128,2,128]{2,1,0:T(2,128)(2,1)} async-done(((bf16[128,2,128]{2,1,0:T(2,128)(2,1)}), bf16[128,2,128]{2,1,0:T(2,128)(2,1)}) %all-reduce.6.cloned.1.call-update) | async-done | bytes 65552
  (108 shorter events, 43.3 us)
Async XLA Ops:
  8.0 18.1 %copy-start = (bf16[12,128,128]{2,1,0:T(8,128)(2,1)S(1)}, bf16[12,128,128]{2,1,0:T(8,128)(2,1)}, u32[]{:S(2)}) copy-start(bf16[12,128,128]{2,1,0:T(8,128)(2,1)} %param.14) | copy-start | bytes 1179652
  9.7 47.5 %all-to-all-start = ((bf16[2,32,16,128]{3,2,0,1:T(8,128)(2,1)}), bf16[2,32,16,128]{3,2,0,1:T(8,128)(2,1)S(1)}, u32[]{:S(2)}, u32[]{:S(2)}) async-start(bf16[2,32,16,128]{3,2,0,1:T(8,128)(2,1)} %copy.116), calls=%async_computation | async-start | bytes 524288 | tf_op jit(solution)/shard_map/all_to_all | solution.py:184
  27.7 1.9 copy-start.17
  31.5 24.6 %copy-start.9 = (bf16[512,128]{1,0:T(8,128)(2,1)S(1)}, bf16[512,128]{1,0:T(8,128)(2,1)}, u32[]{:S(2)}) copy-start(bf16[512,128]{1,0:T(8,128)(2,1)} %param.19) | copy-start | bytes 393220
  31.7 35.3 %copy-start.1 = (bf16[64,16,128]{2,1,0:T(8,128)(2,1)S(1)}, bf16[64,16,128]{2,1,0:T(8,128)(2,1)}, u32[]{:S(2)}) copy-start(bf16[64,16,128]{2,1,0:T(8,128)(2,1)} %param.11) | copy-start | bytes 786436
  31.7 35.3 %copy-start.10 = (bf16[4,128,128]{2,1,0:T(8,128)(2,1)S(1)}, bf16[4,128,128]{2,1,0:T(8,128)(2,1)}, u32[]{:S(2)}) copy-start(bf16[4,128,128]{2,1,0:T(8,128)(2,1)} %param.13) | copy-start | bytes 393220
  57.2 13.6 %copy-start.13 = (bf16[2,128,128]{2,1,0:T(8,128)(2,1)S(1)}, bf16[2,128,128]{2,1,0:T(8,128)(2,1)}, u32[]{:S(2)}) copy-start(bf16[2,128,128]{2,1,0:T(8,128)(2,1)} %param.12) | copy-start | bytes 196612
  57.2 21.5 %all-to-all-start.1 = ((bf16[2,32,16,128]{3,2,0,1:T(8,128)(2,1)}), bf16[2,32,16,128]{3,2,0,1:T(8,128)(2,1)S(1)}, u32[]{:S(2)}, u32[]{:S(2)}) async-start(bf16[2,32,16,128]{3,2,0,1:T(8,128)(2,1)} %copy.121), calls=%async_computation.1 | async-start | bytes 524288 | tf_op jit(solution)/shard_map/all_to_all | solution.py:187
  78.7 2.2 copy-start.7
  93.4 2.9 copy-start.2
  93.4 2.9 copy-start.16
  97.2 1.5 copy-start.3
  98.7 2.7 copy-start.4
  99.9 1.9 copy-start.5
  103.4 3.6 copy-start.11
  113.1 1.8 copy-start.14
  113.1 2.8 copy-start.8
  114.6 2.1 copy-start.6
  117.0 14.8 %all-to-all-start.3 = ((bf16[64,1,16,128]{3,2,1,0:T(8,128)(2,1)}), bf16[64,1,16,128]{3,2,1,0:T(8,128)(2,1)S(1)}, u32[]{:S(2)}, u32[]{:S(2)}) async-start(bf16[64,1,16,128]{3,2,1,0:T(8,128)(2,1)} %bitcast.37), calls=%async_computation.3 | async-start | bytes 524288 | tf_op jit(solution)/shard_map/all_to_all | solution.py:206
  121.4 151.7 %all-reduce.4.cloned.1.call-start = ((), (), s32[]{:S(2)}) async-start(), calls=%async_computation.4 | async-start | bytes 393216 | tf_op jit(solution)/shard_map/psum | solution.py:226
  121.8 0.7 copy-start.12
  131.8 149.3 %all-to-all-start.2 = ((bf16[64,1,16,128]{3,2,1,0:T(8,128)(2,1)}), bf16[64,1,16,128]{3,2,1,0:T(8,128)(2,1)S(1)}, u32[]{:S(2)}, u32[]{:S(2)}) async-start(bf16[64,1,16,128]{3,2,1,0:T(8,128)(2,1)} %bitcast.32), calls=%async_computation.2 | async-start | bytes 524288 | tf_op jit(solution)/shard_map/all_to_all | solution.py:203
  137.0 253.3 %all-reduce.6.cloned.1.call-start = ((), (), s32[]{:S(2)}) async-start(), calls=%async_computation.5 | async-start | bytes 131072
  277.3 1.9 copy-start.18
  (1 other events, 0.6 us)
Sparse Core Ops, SparseCore 0:
  126.0 147.0 all-reduce.3
Sparse Core Ops, SparseCore 1:
  283.4 106.9 all-reduce.5
where the time goes:
time: 401 us; the launch traced here: 400 us
  waiting for transfers between devices  255 us (64%)
  local copies, waits for them, and re-layouts  36.5 us (9%)
  starting transfers between devices  30 us (7%)
  matrix products  27.2 us (7%)
  blocking collectives  24.1 us (6%)
  between operations  17.4 us (4%)
  other arithmetic  10.5 us (3%)
    psum x1, waiting for transfers between devices, local(): lax.psum(partial_grads.astype(jnp.bfloat16), 'config').astype(jnp.float32)  136 us
    unnamed x3, waiting for transfers between devices  106 us
    all_gather x1, blocking collectives, local(): lax.all_gather(local_hubs, 'graph', axis=1, tiled=True)  24.1 us
    all_to_all x1, starting transfers between devices, local(): lax.all_to_all(features.reshape(split_shape), 'config', split_axis=1, con...  10.5 us
    all_to_all x1, starting transfers between devices, local(): lax.all_to_all(aggregate.reshape(split_shape), 'config', split_axis=1, co...  9.81 us
  transfers between devices with their start and end apart: 6, of which 4 were waited for; matrix products, arithmetic and copies ran while one was open for 7% of the time, Pallas kernels for 0%

commit v1 on v0

v1 whole, which is shorter than its diff:
```python
import functools
import math

import jax
import jax.numpy as jnp
from jax import lax
from jax.experimental import pallas as pl
from jax.experimental.pallas import tpu as pltpu
from jax.sharding import PartitionSpec as P

HEADS = 4
CAP = 20.0
F = 128
MESH = pl.DeviceIdType.MESH
BF = jnp.bfloat16
F32 = jnp.float32


def mm(a, b):
    return jnp.dot(a, b, preferred_element_type=F32)


def mm_nt(a, b):
    return lax.dot_general(a, b, (((1,), (1,)), ((), ())), preferred_element_type=F32)


def mm_tn(a, b):
    return lax.dot_general(a, b, (((0,), (0,)), ((), ())), preferred_element_type=F32)


def kernel(
    feat, cot, sw, aw, tiles, dst, src, cnt, ids, hubw,
    lo_out, gf_out, gw_out,
    adj, adj_t, hub_t, fa_t, acc32, dsil, agg, hid, hall, h32, c32, g32, o32,
    dqkv, hn, mixn, cotn, gmn, gsend, gback, gpre, gacat, tot32,
    hubloc, hub_all, hg_src, hg_buf, ars_src, ars_buf, aag_src, aag_buf,
    srs_src, srs_buf, sag_src, sag_buf,
    fwd_s, fwd_r, back_s, back_r, hub_s, hub_r, hg_s, hg_r,
    ars_s, ars_r, aag_s, aag_r, srs_s, srs_r, sag_s, sag_r,
):
    g = lax.axis_index("graph")
    c = lax.axis_index("config")
    n_g = lax.axis_size("graph")
    n_c = lax.axis_size("config")
    barrier = pltpu.get_barrier_semaphore()

    def hello_config(k, carry):
        pl.semaphore_signal(barrier, inc=1, device_id={"config": lax.rem(c + k, n_c)}, device_id_type=MESH)
        return carry

    def hello_graph(k, carry):
        pl.semaphore_signal(barrier, inc=1, device_id={"graph": lax.rem(g + k, n_g)}, device_id_type=MESH)
        return carry

    lax.fori_loop(1, n_g, hello_graph, 0)
    lax.fori_loop(1, n_c, hello_config, 0)

    def send(src_ref, dst_ref, send_sem, recv_sem, where):
        pltpu.make_async_remote_copy(
            src_ref=src_ref, dst_ref=dst_ref, send_sem=send_sem, recv_sem=recv_sem,
            device_id=where, device_id_type=MESH,
        ).start()

    def wait_bytes(ref, sem):
        pltpu.make_async_copy(ref, ref, sem).wait()

    base = g * 512
    row = lax.broadcasted_iota(jnp.int32, (16, 512), 0)
    col = lax.broadcasted_iota(jnp.int32, (16, 512), 1)
    want = jnp.full((16, 512), -1, jnp.int32)
    for j in range(8):
        want = jnp.where(row == j, ids[j] - base, want)
    onehot = jnp.where(col == want, 1.0, 0.0).astype(BF)
    x_cat = jnp.concatenate([feat[0], feat[1]], axis=1)
    rows_hub = mm(onehot, x_cat)
    hubloc[...] = jnp.concatenate([rows_hub[:8, :F], rows_hub[:8, F:]], axis=0).astype(BF)

    pl.semaphore_wait(barrier, n_g + n_c - 2)

    pltpu.make_async_copy(hubloc, hub_all.at[g], hub_r).start()

    def send_hub(k, carry):
        send(hubloc, hub_all.at[g], hub_s, hub_r, {"graph": lax.rem(g + k, n_g)})
        return carry

    lax.fori_loop(1, n_g, send_hub, 0)

    def build(b, carry):
        at = pl.multiple_of(b * 128, 128)
        for s in range(4):
            acc = jnp.zeros((128, 128), F32)
            for t in range(12):
                live = (dst[t] == b) & (src[t] == s) & (t < cnt[0])
                acc = acc + jnp.where(live, 1.0, 0.0) * tiles[t].astype(F32)
            adj[pl.ds(at, 128), s * 128 : (s + 1) * 128] = acc.astype(BF)
            adj_t[s * 128 : (s + 1) * 128, pl.ds(at, 128)] = acc.T.astype(BF)
        return carry

    lax.fori_loop(0, 4, build, 0)

    def first(b, carry):
        rows = pl.ds(pl.multiple_of(b * 128, 128), 128)
        acc32[rows, :] = mm(adj[rows, :], jnp.concatenate([feat[0], feat[1]], axis=1))
        return carry

    lax.fori_loop(0, 4, first, 0)

    wait_bytes(hub_all, hub_r)
    hubs = hub_all[...].astype(F32).reshape(16, 2, 8, F)
    hub_cat = jnp.concatenate(
        [hubs[:, 0].reshape(128, F).astype(BF), hubs[:, 1].reshape(128, F).astype(BF)], axis=1
    )
    w_sage = sw[...].reshape(2 * F, F)

    def forward(i, carry):
        b = lax.rem(c // 8 + i, 4)
        rows = pl.ds(pl.multiple_of(b * 128, 128), 128)
        acc = acc32[rows, :] + mm(hubw[rows, :], hub_cat)
        for l in range(2):
            a_l = acc[:, l * F : (l + 1) * F].astype(BF)
            agg[l, rows, :] = a_l
            pre = mm(jnp.concatenate([feat[l, rows, :], a_l], axis=1), w_sage)
            sig = 1.0 / (1.0 + jnp.exp(-pre))
            dsil[l, rows, :] = sig * (1.0 + pre * (1.0 - sig))
            hid[l, rows, :] = (pre * sig).astype(BF)

        def send_hidden(k, inner):
            p = b * 8 + lax.rem(c + k, 8)
            piece = hid.at[:, pl.ds(pl.multiple_of(p * 16, 16), 16), :]

            @pl.when(p != c)
            def _():
                send(piece, hall.at[pl.ds(c * 2, 2)], fwd_s, fwd_r, {"config": p})

            @pl.when(p == c)
            def _():
                pltpu.make_async_copy(piece, hall.at[pl.ds(c * 2, 2)], fwd_r).start()

            return inner

        lax.fori_loop(0, 8, send_hidden, 0)
        return carry

    lax.fori_loop(0, 4, forward, 0)

    c32[...] = cot[...].astype(F32).reshape(1024, F)

    def cot_nodes(i, carry):
        rows = pl.ds(pl.multiple_of(i * 256, 256), 256)
        part = jnp.concatenate(
            [c32[pl.ds(i * 4 + k, 64, stride=16), :] for k in range(4)], axis=0
        ).astype(BF)
        cotn[rows, :] = part
        gmn[rows, :] = mm_nt(part, aw[3]).astype(BF)
        return carry

    lax.fori_loop(0, 4, cot_nodes, 0)

    hub_t[...] = hubw[...].astype(F32).T.astype(BF)
    for l in range(2):
        fa_t[0:F, l * 512 : (l + 1) * 512] = feat[l].astype(F32).T.astype(BF)
        fa_t[F : 2 * F, l * 512 : (l + 1) * 512] = agg[l].astype(F32).T.astype(BF)

    wait_bytes(hall, fwd_r)
    h32[...] = hall[...].astype(F32).reshape(1024, F)

    w_qkv = jnp.concatenate([aw[0], aw[1], aw[2]], axis=1)

    def head_of(shape, dim, width):
        return lax.broadcasted_iota(jnp.int32, shape, dim) // width

    head_mask = jnp.where(
        head_of((256, F), 0, 64) == head_of((256, F), 1, 32), 1.0, 0.0
    ).astype(BF)
    ones_mm = jnp.where(
        head_of((256, 256), 0, 64) == head_of((256, 256), 1, 64), 1.0, 0.0
    ).astype(BF)
    ones_dm = jnp.where(
        head_of((F, 256), 0, 32) == head_of((F, 256), 1, 64), 1.0, 0.0
    ).astype(BF)
    lane = lax.broadcasted_iota(jnp.int32, (64, F), 1)

    def own_head(full):
        return jnp.where(
            lane < 64,
            jnp.where(lane < 32, full[0:64], full[64:128]),
            jnp.where(lane < 96, full[128:192], full[192:256]),
        )

    root = 1.0 / math.sqrt(32.0)

    def attend(i, carry):
        rows = pl.ds(pl.multiple_of(i * 256, 256), 256)
        h_four = jnp.concatenate([h32[pl.ds(i * 4 + k, 64, stride=16), :] for k in range(4)], axis=0)
        h_b = h_four.astype(BF)
        hn[rows, :] = h_b
        qkv = mm(h_b, w_qkv).astype(BF)
        mixes, d_q, d_k, d_v = [], [], [], []
        for k in range(4):
            q = qkv[k * 64 : (k + 1) * 64, 0:F]
            key = qkv[k * 64 : (k + 1) * 64, F : 2 * F]
            val = qkv[k * 64 : (k + 1) * 64, 2 * F : 3 * F]
            gm = gmn[pl.ds(pl.multiple_of(i * 256 + k * 64, 64), 64), :]
            key_x = jnp.concatenate([key] * 4, axis=0) * head_mask
            val_x = jnp.concatenate([val] * 4, axis=0) * head_mask
            t = jnp.tanh(mm_nt(q, key_x) * (root / CAP))
            w = jnp.exp(CAP * t)
            den = mm(w.astype(BF), ones_mm)
            p_b = (w / den).astype(BF)
            mix = mm(p_b, val_x)
            dp = mm_nt(gm, val_x)
            delta = mm((gm.astype(F32) * mix).astype(BF), ones_dm)
            ds = (p_b.astype(F32) * (dp - delta) * ((1.0 - t * t) * root)).astype(BF)
            mixes.append(mix.astype(BF))
            d_q.append(mm(ds, key_x).astype(BF))
            d_k.append(own_head(mm_tn(ds, q)).astype(BF))
            d_v.append(own_head(mm_tn(p_b, gm)).astype(BF))
        mix_b = jnp.concatenate(mixes, axis=0)
        mixn[rows, :] = mix_b
        grads = jnp.concatenate(
            [jnp.concatenate(d_q, axis=0), jnp.concatenate(d_k, axis=0), jnp.concatenate(d_v, axis=0)],
            axis=1,
        )
        dqkv[rows, :] = grads
        out = h_four + mm(mix_b, aw[3])
        back = cotn[rows, :].astype(F32) + mm_nt(grads, w_qkv)
        for k in range(4):
            o32[pl.ds(i * 4 + k, 64, stride=16), :] = out[k * 64 : (k + 1) * 64]
            g32[pl.ds(i * 4 + k, 64, stride=16), :] = back[k * 64 : (k + 1) * 64]
        return carry

    lax.fori_loop(0, 4, attend, 0)
    gsend[...] = g32[...].reshape(64, 16, F).astype(BF)

    def send_back(k, carry):
        p = lax.rem(c + k, n_c)
        send(
            gsend.at[pl.ds(p * 2, 2)],
            gback.at[:, pl.ds(pl.multiple_of(c * 16, 16), 16), :],
            back_s, back_r, {"config": p},
        )
        return carry

    pltpu.make_async_copy(
        gsend.at[pl.ds(c * 2, 2)], gback.at[:, pl.ds(pl.multiple_of(c * 16, 16), 16), :], back_r
    ).start()
    lax.fori_loop(1, n_c, send_back, 0)

    lo_out[...] = o32[...].reshape(64, 16, F).astype(BF)
    part_qkv = mm_tn(hn[...], dqkv[...])
    part_o = mm_tn(mixn[...], cotn[...])
    for i in range(3):
        ars_src[i * 8 : (i + 1) * 8] = part_qkv[:, i * F : (i + 1) * F].reshape(8, 16, F).astype(BF)
    ars_src[24:32] = part_o.reshape(8, 16, F).astype(BF)

    def send_attn(k, carry):
        p = lax.rem(c + k, n_c)
        send(ars_src.at[p], ars_buf.at[c], ars_s, ars_r, {"config": p})
        return carry

    pltpu.make_async_copy(ars_src.at[c], ars_buf.at[c], ars_r).start()
    lax.fori_loop(1, n_c, send_attn, 0)

    wait_bytes(gback, back_r)

    def backward(b, carry):
        rows = pl.ds(pl.multiple_of(b * 128, 128), 128)
        for l in range(2):
            gp = (gback[l, rows, :].astype(F32) * dsil[l, rows, :]).astype(BF)
            gpre[pl.ds(pl.multiple_of(l * 512 + b * 128, 128), 128), :] = gp
            both = mm_nt(gp, w_sage)
            tot32[rows, l * F : (l + 1) * F] = both[:, :F]
            gacat[rows, l * F : (l + 1) * F] = both[:, F:].astype(BF)
        return carry

    lax.fori_loop(0, 4, backward, 0)

    srs_src[...] = mm(fa_t[...], gpre[...]).reshape(16, 16, F).astype(BF)

    def send_sage(k, carry):
        q = lax.rem(c // 2 + k, 16)
        p = q * 2

        @pl.when(p != c)
        def _():
            send(srs_src.at[q], srs_buf.at[c], srs_s, srs_r, {"config": p})

        @pl.when(p == c)
        def _():
            pltpu.make_async_copy(srs_src.at[q], srs_buf.at[c], srs_r).start()

        return carry

    lax.fori_loop(0, 16, send_sage, 0)

    hub_part = mm(hub_t[...], gacat[...])
    hg_src[...] = jnp.concatenate(
        [hub_part[:, :F].reshape(16, 8, F), hub_part[:, F:].reshape(16, 8, F)], axis=1
    ).astype(BF)

    def send_hub_grad(k, carry):
        s = lax.rem(g + k, n_g)
        send(hg_src.at[s], hg_buf.at[g], hg_s, hg_r, {"graph": s})
        return carry

    pltpu.make_async_copy(hg_src.at[g], hg_buf.at[g], hg_r).start()
    lax.fori_loop(1, n_g, send_hub_grad, 0)

    wait_bytes(ars_buf, ars_r)
    aag_src[...] = jnp.sum(ars_buf[...].astype(F32), axis=0).astype(BF)
    pltpu.make_async_copy(aag_src, aag_buf.at[c], aag_r).start()

    def send_attn_sum(k, carry):
        send(aag_src, aag_buf.at[c], aag_s, aag_r, {"config": lax.rem(c + k, n_c)})
        return carry

    lax.fori_loop(1, n_c, send_attn_sum, 0)

    @pl.when(lax.rem(c, 2) == 0)
    def _():
        wait_bytes(srs_buf, srs_r)
        sag_src[...] = jnp.sum(srs_buf[...].astype(F32), axis=0).astype(BF)
        pltpu.make_async_copy(sag_src, sag_buf.at[c // 2], sag_r).start()

        def send_sage_sum(k, carry):
            send(sag_src, sag_buf.at[c // 2], sag_s, sag_r, {"config": lax.rem(c + k, n_c)})
            return carry

        lax.fori_loop(1, n_c, send_sage_sum, 0)

    def back_rows(b, carry):
        rows = pl.ds(pl.multiple_of(b * 128, 128), 128)
        tot32[rows, :] = tot32[rows, :] + mm(adj_t[rows, :], gacat[...])
        return carry

    lax.fori_loop(0, 4, back_rows, 0)

    lane_id = lax.broadcasted_iota(jnp.int32, (512, F), 1)
    node_id = lax.broadcasted_iota(jnp.int32, (512, F), 0)
    want_t = jnp.full((512, F), -1, jnp.int32)
    for j in range(8):
        want_t = jnp.where((lane_id == j) | (lane_id == j + 8), ids[j] - base, want_t)
    onehot_t = jnp.where(node_id == want_t, 1.0, 0.0).astype(BF)

    wait_bytes(hg_buf, hg_r)
    hub_sum = jnp.sum(hg_buf[...].astype(F32), axis=0)
    hub_both = jnp.concatenate([hub_sum[0:8], hub_sum[8:16]], axis=1)
    high = hub_both.astype(BF).astype(F32)
    hub_mat = jnp.concatenate([high, hub_both - high, jnp.zeros((112, 256), F32)], axis=0).astype(BF)
    total = (tot32[...] + mm(onehot_t, hub_mat)).astype(BF)
    gf_out[0] = total[:, :F]
    gf_out[1] = total[:, F:]

    scale = 1.0 / math.sqrt(64 * 512)
    wait_bytes(aag_buf, aag_r)
    for i in range(4):
        gw_out[0, 2 + i] = aag_buf[i * 8 : (i + 1) * 8].astype(F32).reshape(F, F) * scale
    wait_bytes(sag_buf, sag_r)
    for i in range(2):
        gw_out[0, i] = sag_buf[i * 8 : (i + 1) * 8].astype(F32).reshape(F, F) * scale

    wait_bytes(hub_all.at[pl.ds(0, 15)], hub_s)
    wait_bytes(hall.at[pl.ds(0, 62)], fwd_s)
    wait_bytes(gsend.at[pl.ds(0, 62)], back_s)
    wait_bytes(ars_buf.at[pl.ds(0, 31)], ars_s)
    wait_bytes(hg_buf.at[pl.ds(0, 15)], hg_s)
    wait_bytes(aag_buf.at[pl.ds(0, 31)], aag_s)

    @pl.when(lax.rem(c, 2) == 0)
    def _():
        wait_bytes(srs_buf.at[pl.ds(0, 15)], srs_s)
        wait_bytes(aag_buf.at[pl.ds(0, 31)], sag_s)

    @pl.when(lax.rem(c, 2) == 1)
    def _():
        wait_bytes(srs_buf.at[pl.ds(0, 16)], srs_s)


def local(features, cotangent, sage_weight, attn_weight, tile_vals, tile_dst, tile_src, tile_count, hub_ids, hub_weight):
    vmem = pl.BlockSpec(memory_space=pltpu.VMEM)
    smem = pl.BlockSpec(memory_space=pltpu.SMEM)
    v = pltpu.VMEM
    return pl.pallas_call(
        kernel,
        out_shape=(
            jax.ShapeDtypeStruct((64, 16, F), BF),
            jax.ShapeDtypeStruct((2, 512, F), BF),
            jax.ShapeDtypeStruct((1, 6, F, F), F32),
        ),
        in_specs=[vmem] * 5 + [smem] * 4 + [vmem],
        out_specs=(vmem, vmem, vmem),
        scratch_shapes=[
            v((512, 512), BF),
            v((512, 512), BF),
            v((128, 512), BF),
            v((256, 1024), BF),
            v((512, 256), F32),
            v((2, 512, F), F32),
            v((2, 512, F), BF),
            v((2, 512, F), BF),
            v((64, 16, F), BF),
            v((1024, F), F32),
            v((1024, F), F32),
            v((1024, F), F32),
            v((1024, F), F32),
            v((1024, 384), BF),
            v((1024, F), BF),
            v((1024, F), BF),
            v((1024, F), BF),
            v((1024, F), BF),
            v((64, 16, F), BF),
            v((2, 512, F), BF),
            v((1024, F), BF),
            v((512, 256), BF),
            v((512, 256), F32),
            v((16, F), BF),
            v((16, 16, F), BF),
            v((16, 16, F), BF),
            v((16, 16, F), BF),
            v((32, 16, F), BF),
            v((32, 16, F), BF),
            v((16, F), BF),
            v((32, 16, F), BF),
            v((16, 16, F), BF),
            v((32, 16, F), BF),
            v((16, F), BF),
            v((16, 16, F), BF),
        ]
        + [pltpu.SemaphoreType.DMA] * 16,
        compiler_params=pltpu.CompilerParams(
            collective_id=0, has_side_effects=True, vmem_limit_bytes=40 * 2**20
        ),
    )(features, cotangent, sage_weight, attn_weight, tile_vals, tile_dst, tile_src, tile_count, hub_ids, hub_weight)


def solution(mesh):
    return jax.shard_map(
        local,
        mesh=mesh,
        in_specs=(
            P("config", "graph", None),
            P(None, ("graph", "config"), None),
            P(),
            P(),
            P("graph", None, None),
            P("graph"),
            P("graph"),
            P("graph"),
            P("graph"),
            P("graph", None),
        ),
        out_specs=(
            P(None, ("graph", "config"), None),
            P("config", "graph", None),
            P("graph", None, None, None),
        ),
        check_vma=False,
    )
```

time: 401 us -> 77.6 us (0.19)
  the two profiles are of different devices: /device:TPU:1 before, /device:TPU:16 now
where the time goes in v1:
time: 77.6 us; the launch traced here: 77.3 us
  Pallas kernels  68.3 us (88%)
  local copies, waits for them, and re-layouts  7.7 us (10%)
  between operations  1.37 us (2%)
    pallas_call x1, Pallas kernels, local(): pl.pallas_call(kernel, out_shape=(jax.ShapeDtypeStruct((64, 16, F), BF),...  68.3 us
    unnamed x21, local copies, waits for them, and re-layouts  7.7 us

profile of v1, /device:TPU:16, one launch (start us, length us, event | category | flops | bytes accessed | tf_op | source)
XLA Modules:
  0.0 77.3 jit_solution(15359033057238041506)
XLA Ops:
  0.6 0.0 copy-start.8
  0.6 0.0 copy-start.7
  0.7 0.0 copy-start.6
  1.3 0.0 copy-done.8
  1.3 0.0 copy-done.7
  1.4 0.0 copy-done.6
  1.4 0.0 copy-start
  1.4 1.0 %copy-done = bf16[12,128,128]{2,1,0:T(8,128)(2,1)S(1)} copy-done((bf16[12,128,128]{2,1,0:T(8,128)(2,1)S(1)}, bf16[12,128,128]{2,1,0:T(8,128)(2,1)}, u32[]{:S(2)}) %copy-start) | copy-done | bytes 393240
  2.4 0.0 copy-start.1
  2.4 0.9 %copy-done.1 = bf16[2,512,128]{2,1,0:T(8,128)(2,1)S(1)} copy-done((bf16[2,512,128]{2,1,0:T(8,128)(2,1)S(1)}, bf16[2,512,128]{2,1,0:T(8,128)(2,1)}, u32[]{:S(2)}) %copy-start.1) | copy-done | bytes 262168
  3.3 0.0 copy-start.2
  3.3 0.9 %copy-done.2 = bf16[64,16,128]{2,1,0:T(8,128)(2,1)S(1)} copy-done((bf16[64,16,128]{2,1,0:T(8,128)(2,1)S(1)}, bf16[64,16,128]{2,1,0:T(8,128)(2,1)}, u32[]{:S(2)}) %copy-start.2) | copy-done | bytes 262168
  4.3 0.0 copy-start.3
  4.3 0.9 %copy-done.3 = bf16[4,128,128]{2,1,0:T(8,128)(2,1)S(1)} copy-done((bf16[4,128,128]{2,1,0:T(8,128)(2,1)S(1)}, bf16[4,128,128]{2,1,0:T(8,128)(2,1)}, u32[]{:S(2)}) %copy-start.3) | copy-done | bytes 131096
  5.2 0.0 copy-start.4
  5.2 0.9 %copy-done.4 = bf16[512,128]{1,0:T(8,128)(2,1)S(1)} copy-done((bf16[512,128]{1,0:T(8,128)(2,1)S(1)}, bf16[512,128]{1,0:T(8,128)(2,1)}, u32[]{:S(2)}) %copy-start.4) | copy-done | bytes 131096
  6.1 0.0 copy-start.5
  6.1 0.8 %copy-done.5 = bf16[2,128,128]{2,1,0:T(8,128)(2,1)S(1)} copy-done((bf16[2,128,128]{2,1,0:T(8,128)(2,1)S(1)}, bf16[2,128,128]{2,1,0:T(8,128)(2,1)}, u32[]{:S(2)}) %copy-start.5) | copy-done | bytes 65560
  6.9 68.3 %shard_map.121 = (bf16[64,16,128]{2,1,0:T(8,128)(2,1)S(1)}, bf16[2,512,128]{2,1,0:T(8,128)(2,1)S(1)}, f32[1,6,128,128]{3,2,1,0:T(8,128)S(1)}) custom-call(bf16[2,512,128]{2,1,0:T(8,128)(2,1)S(1)} %copy-done.1, bf16[64,16,128]{2,1,0:T(8,128)(2,1)S(1)} %copy-done.2, bf16[2,128,128]{2,1,0:T(8,128)(2,1)S(1)} %copy-done.5, bf16[4,128,128]{2,1,0:T(8,128)(2,1)S(1)} %copy-done.3, ...), custom_call_target="tpu_custom_call" | custom-call | tf_op jit(solution)/shard_map/pallas_call | solution.py:383
  75.2 0.7 copy.17
  75.9 0.7 copy.18
  76.6 0.7 copy.19
Async XLA Ops:
  0.6 0.7 copy-start.8
  0.6 0.7 copy-start.7
  0.7 0.7 copy-start.6
  1.4 1.0 %copy-start = (bf16[12,128,128]{2,1,0:T(8,128)(2,1)S(1)}, bf16[12,128,128]{2,1,0:T(8,128)(2,1)}, u32[]{:S(2)}) copy-start(bf16[12,128,128]{2,1,0:T(8,128)(2,1)} %tiles.1) | copy-start | bytes 1179652
  2.4 0.9 %copy-start.1 = (bf16[2,512,128]{2,1,0:T(8,128)(2,1)S(1)}, bf16[2,512,128]{2,1,0:T(8,128)(2,1)}, u32[]{:S(2)}) copy-start(bf16[2,512,128]{2,1,0:T(8,128)(2,1)} %feat.1) | copy-start | bytes 786436
  3.3 0.9 %copy-start.2 = (bf16[64,16,128]{2,1,0:T(8,128)(2,1)S(1)}, bf16[64,16,128]{2,1,0:T(8,128)(2,1)}, u32[]{:S(2)}) copy-start(bf16[64,16,128]{2,1,0:T(8,128)(2,1)} %cot.1) | copy-start | bytes 786436
  4.3 0.9 %copy-start.3 = (bf16[4,128,128]{2,1,0:T(8,128)(2,1)S(1)}, bf16[4,128,128]{2,1,0:T(8,128)(2,1)}, u32[]{:S(2)}) copy-start(bf16[4,128,128]{2,1,0:T(8,128)(2,1)} %aw.1) | copy-start | bytes 393220
  5.2 0.9 %copy-start.4 = (bf16[512,128]{1,0:T(8,128)(2,1)S(1)}, bf16[512,128]{1,0:T(8,128)(2,1)}, u32[]{:S(2)}) copy-start(bf16[512,128]{1,0:T(8,128)(2,1)} %hubw.1) | copy-start | bytes 393220
  6.1 0.8 %copy-start.5 = (bf16[2,128,128]{2,1,0:T(8,128)(2,1)S(1)}, bf16[2,128,128]{2,1,0:T(8,128)(2,1)}, u32[]{:S(2)}) copy-start(bf16[2,128,128]{2,1,0:T(8,128)(2,1)} %sw.1) | copy-start | bytes 196612

commit v2 on v1

--- a/solution.py
+++ b/solution.py
@@ -29,19 +29,28 @@
 
 
 def kernel(
-    feat, cot, sw, aw, tiles, dst, src, cnt, ids, hubw,
-    lo_out, gf_out, gw_out,
+    feat_h, cot_h, sw_h, aw_h, tiles_h, dst, src, cnt, ids, hubw_h,
+    lo_h, gf_h, gw_h,
+    feat, cot, sw, aw, tiles, hubw, lo_out, gf_out, gw_out,
     adj, adj_t, hub_t, fa_t, acc32, dsil, agg, hid, hall, h32, c32, g32, o32,
     dqkv, hn, mixn, cotn, gmn, gsend, gback, gpre, gacat, tot32,
     hubloc, hub_all, hg_src, hg_buf, ars_src, ars_buf, aag_src, aag_buf,
     srs_src, srs_buf, sag_src, sag_buf,
     fwd_s, fwd_r, back_s, back_r, hub_s, hub_r, hg_s, hg_r,
-    ars_s, ars_r, aag_s, aag_r, srs_s, srs_r, sag_s, sag_r,
+    ars_s, ars_r, aag_s, aag_r, srs_s, srs_r, sag_s, sag_r, in_sem, out_sem,
 ):
     g = lax.axis_index("graph")
     c = lax.axis_index("config")
     n_g = lax.axis_size("graph")
     n_c = lax.axis_size("config")
+    loads = [
+        pltpu.make_async_copy(a, b, in_sem.at[i])
+        for i, (a, b) in enumerate(
+            ((feat_h, feat), (tiles_h, tiles), (hubw_h, hubw), (sw_h, sw), (cot_h, cot), (aw_h, aw))
+        )
+    ]
+    for load in loads:
+        load.start()
     barrier = pltpu.get_barrier_semaphore()
 
     def hello_config(k, carry):
@@ -60,6 +69,9 @@
             src_ref=src_ref, dst_ref=dst_ref, send_sem=send_sem, recv_sem=recv_sem,
             device_id=where, device_id_type=MESH,
         ).start()
+
+    def keep(src_ref, dst_ref, sem):
+        pltpu.make_async_copy(src_ref, dst_ref, sem).start()
 
     def wait_bytes(ref, sem):
         pltpu.make_async_copy(ref, ref, sem).wait()
@@ -71,19 +83,23 @@
     for j in range(8):
         want = jnp.where(row == j, ids[j] - base, want)
     onehot = jnp.where(col == want, 1.0, 0.0).astype(BF)
+    loads[0].wait()
     x_cat = jnp.concatenate([feat[0], feat[1]], axis=1)
     rows_hub = mm(onehot, x_cat)
     hubloc[...] = jnp.concatenate([rows_hub[:8, :F], rows_hub[:8, F:]], axis=0).astype(BF)
 
     pl.semaphore_wait(barrier, n_g + n_c - 2)
 
-    pltpu.make_async_copy(hubloc, hub_all.at[g], hub_r).start()
+    keep(hubloc, hub_all.at[g], hub_r)
 
     def send_hub(k, carry):
         send(hubloc, hub_all.at[g], hub_s, hub_r, {"graph": lax.rem(g + k, n_g)})
         return carry
 
     lax.fori_loop(1, n_g, send_hub, 0)
+
+    for load in loads[1:]:
+        load.wait()
 
     def build(b, carry):
         at = pl.multiple_of(b * 128, 128)
@@ -134,7 +150,7 @@
 
             @pl.when(p == c)
             def _():
-                pltpu.make_async_copy(piece, hall.at[pl.ds(c * 2, 2)], fwd_r).start()
+                keep(piece, hall.at[pl.ds(c * 2, 2)], fwd_r)
 
             return inner
 
@@ -172,12 +188,7 @@
     head_mask = jnp.where(
         head_of((256, F), 0, 64) == head_of((256, F), 1, 32), 1.0, 0.0
     ).astype(BF)
-    ones_mm = jnp.where(
-        head_of((256, 256), 0, 64) == head_of((256, 256), 1, 64), 1.0, 0.0
-    ).astype(BF)
-    ones_dm = jnp.where(
-        head_of((F, 256), 0, 32) == head_of((F, 256), 1, 64), 1.0, 0.0
-    ).astype(BF)
+    zeros = jnp.zeros((64, F), BF)
     lane = lax.broadcasted_iota(jnp.int32, (64, F), 1)
 
     def own_head(full):
@@ -195,26 +206,37 @@
         h_b = h_four.astype(BF)
         hn[rows, :] = h_b
         qkv = mm(h_b, w_qkv).astype(BF)
-        mixes, d_q, d_k, d_v = [], [], [], []
-        for k in range(4):
-            q = qkv[k * 64 : (k + 1) * 64, 0:F]
-            key = qkv[k * 64 : (k + 1) * 64, F : 2 * F]
-            val = qkv[k * 64 : (k + 1) * 64, 2 * F : 3 * F]
-            gm = gmn[pl.ds(pl.multiple_of(i * 256 + k * 64, 64), 64), :]
-            key_x = jnp.concatenate([key] * 4, axis=0) * head_mask
-            val_x = jnp.concatenate([val] * 4, axis=0) * head_mask
-            t = jnp.tanh(mm_nt(q, key_x) * (root / CAP))
-            w = jnp.exp(CAP * t)
-            den = mm(w.astype(BF), ones_mm)
-            p_b = (w / den).astype(BF)
-            mix = mm(p_b, val_x)
-            dp = mm_nt(gm, val_x)
-            delta = mm((gm.astype(F32) * mix).astype(BF), ones_dm)
-            ds = (p_b.astype(F32) * (dp - delta) * ((1.0 - t * t) * root)).astype(BF)
-            mixes.append(mix.astype(BF))
-            d_q.append(mm(ds, key_x).astype(BF))
-            d_k.append(own_head(mm_tn(ds, q)).astype(BF))
-            d_v.append(own_head(mm_tn(p_b, gm)).astype(BF))
+        four = range(4)
+        q = [qkv[k * 64 : (k + 1) * 64, 0:F] for k in four]
+        key_x = [jnp.concatenate([qkv[k * 64 : (k + 1) * 64, F : 2 * F]] * 4, axis=0) * head_mask for k in four]
+        val_x = [
+            jnp.concatenate(
+                [jnp.concatenate([qkv[k * 64 : (k + 1) * 64, 2 * F : 3 * F]] * 4, axis=0) * head_mask, head_mask],
+                axis=1,
+            )
+            for k in four
+        ]
+        t = [jnp.tanh(mm_nt(q[k], key_x[k]) * (root / CAP)) for k in four]
+        w = [jnp.exp(CAP * t[k]).astype(BF) for k in four]
+        both = [mm(w[k], val_x[k]) for k in four]
+        inv = [1.0 / both[k][:, F:] for k in four]
+        mix = [both[k][:, :F] * inv[k] for k in four]
+        gm = [gmn[pl.ds(pl.multiple_of(i * 256 + k * 64, 64), 64), :].astype(F32) * inv[k] for k in four]
+        gm_b = [gm[k].astype(BF) for k in four]
+        less = [(-(gm_b[k].astype(F32) * mix[k])).astype(BF) for k in four]
+        dp = [mm_nt(jnp.concatenate([gm_b[k], less[k]], axis=1), val_x[k]) for k in four]
+        ds = [(w[k].astype(F32) * dp[k] * ((1.0 - t[k] * t[k]) * root)).astype(BF) for k in four]
+        d_q = [mm(ds[k], key_x[k]).astype(BF) for k in four]
+        right = [
+            jnp.concatenate(
+                [jnp.concatenate([q[k], zeros], axis=1), jnp.concatenate([zeros, gm_b[k]], axis=1)], axis=0
+            )
+            for k in four
+        ]
+        d_kv = [mm_tn(jnp.concatenate([ds[k], w[k]], axis=0), right[k]) for k in four]
+        d_k = [own_head(d_kv[k][:, :F]).astype(BF) for k in four]
+        d_v = [own_head(d_kv[k][:, F:]).astype(BF) for k in four]
+        mixes = [mix[k].astype(BF) for k in four]
         mix_b = jnp.concatenate(mixes, axis=0)
         mixn[rows, :] = mix_b
         grads = jnp.concatenate(
@@ -241,12 +263,12 @@
         )
         return carry
 
-    pltpu.make_async_copy(
-        gsend.at[pl.ds(c * 2, 2)], gback.at[:, pl.ds(pl.multiple_of(c * 16, 16), 16), :], back_r
-    ).start()
+    keep(gsend.at[pl.ds(c * 2, 2)], gback.at[:, pl.ds(pl.multiple_of(c * 16, 16), 16), :], back_r)
     lax.fori_loop(1, n_c, send_back, 0)
 
     lo_out[...] = o32[...].reshape(64, 16, F).astype(BF)
+    store_lo = pltpu.make_async_copy(lo_out, lo_h, out_sem.at[0])
+    store_lo.start()
     part_qkv = mm_tn(hn[...], dqkv[...])
     part_o = mm_tn(mixn[...], cotn[...])
     for i in range(3):
@@ -258,7 +280,7 @@
         send(ars_src.at[p], ars_buf.at[c], ars_s, ars_r, {"config": p})
         return carry
 
-    pltpu.make_async_copy(ars_src.at[c], ars_buf.at[c], ars_r).start()
+    keep(ars_src.at[c], ars_buf.at[c], ars_r)
     lax.fori_loop(1, n_c, send_attn, 0)
 
     wait_bytes(gback, back_r)
@@ -287,7 +309,7 @@
 
         @pl.when(p == c)
         def _():
-            pltpu.make_async_copy(srs_src.at[q], srs_buf.at[c], srs_r).start()
+            keep(srs_src.at[q], srs_buf.at[c], srs_r)
 
         return carry
 
@@ -303,12 +325,12 @@
         send(hg_src.at[s], hg_buf.at[g], hg_s, hg_r, {"graph": s})
         return carry
 
-    pltpu.make_async_copy(hg_src.at[g], hg_buf.at[g], hg_r).start()
+    keep(hg_src.at[g], hg_buf.at[g], hg_r)
     lax.fori_loop(1, n_g, send_hub_grad, 0)
 
     wait_bytes(ars_buf, ars_r)
     aag_src[...] = jnp.sum(ars_buf[...].astype(F32), axis=0).astype(BF)
-    pltpu.make_async_copy(aag_src, aag_buf.at[c], aag_r).start()
+    keep(aag_src, aag_buf.at[c], aag_r)
 
     def send_attn_sum(k, carry):
         send(aag_src, aag_buf.at[c], aag_s, aag_r, {"config": lax.rem(c + k, n_c)})
@@ -320,7 +342,7 @@
     def _():
         wait_bytes(srs_buf, srs_r)
         sag_src[...] = jnp.sum(srs_buf[...].astype(F32), axis=0).astype(BF)
-        pltpu.make_async_copy(sag_src, sag_buf.at[c // 2], sag_r).start()
+        keep(sag_src, sag_buf.at[c // 2], sag_r)
 
         def send_sage_sum(k, carry):
             send(sag_src, sag_buf.at[c // 2], sag_s, sag_r, {"config": lax.rem(c + k, n_c)})
@@ -350,6 +372,8 @@
     total = (tot32[...] + mm(onehot_t, hub_mat)).astype(BF)
     gf_out[0] = total[:, :F]
     gf_out[1] = total[:, F:]
+    store_gf = pltpu.make_async_copy(gf_out, gf_h, out_sem.at[1])
+    store_gf.start()
 
     scale = 1.0 / math.sqrt(64 * 512)
     wait_bytes(aag_buf, aag_r)
@@ -359,6 +383,9 @@
     for i in range(2):
         gw_out[0, i] = sag_buf[i * 8 : (i + 1) * 8].astype(F32).reshape(F, F) * scale
 
+    store_gw = pltpu.make_async_copy(gw_out, gw_h, out_sem.at[2])
+    store_gw.start()
+
     wait_bytes(hub_all.at[pl.ds(0, 15)], hub_s)
     wait_bytes(hall.at[pl.ds(0, 62)], fwd_s)
     wait_bytes(gsend.at[pl.ds(0, 62)], back_s)
@@ -375,10 +402,14 @@
     def _():
         wait_bytes(srs_buf.at[pl.ds(0, 16)], srs_s)
 
+    store_lo.wait()
+    store_gf.wait()
+    store_gw.wait()
+
 
 def local(features, cotangent, sage_weight, attn_weight, tile_vals, tile_dst, tile_src, tile_count, hub_ids, hub_weight):
-    vmem = pl.BlockSpec(memory_space=pltpu.VMEM)
     smem = pl.BlockSpec(memory_space=pltpu.SMEM)
+    hbm = pl.BlockSpec(memory_space=pltpu.HBM)
     v = pltpu.VMEM
     return pl.pallas_call(
         kernel,
@@ -387,9 +418,18 @@
             jax.ShapeDtypeStruct((2, 512, F), BF),
             jax.ShapeDtypeStruct((1, 6, F, F), F32),
         ),
-        in_specs=[vmem] * 5 + [smem] * 4 + [vmem],
-        out_specs=(vmem, vmem, vmem),
+        in_specs=[hbm] * 5 + [smem] * 4 + [hbm],
+        out_specs=(hbm, hbm, hbm),
         scratch_shapes=[
+            v((2, 512, F), BF),
+            v((64, 16, F), BF),
+            v((2, F, F), BF),
+            v((4, F, F), BF),
+            v((12, F, F), BF),
+            v((512, F), BF),
+            v((64, 16, F), BF),
+            v((2, 512, F), BF),
+            v((1, 6, F, F), F32),
             v((512, 512), BF),
             v((512, 512), BF),
             v((128, 512), BF),
@@ -426,9 +466,10 @@
             v((16, F), BF),
             v((16, 16, F), BF),
         ]
-        + [pltpu.SemaphoreType.DMA] * 16,
+        + [pltpu.SemaphoreType.DMA] * 16
+        + [pltpu.SemaphoreType.DMA((6,)), pltpu.SemaphoreType.DMA((3,))],
         compiler_params=pltpu.CompilerParams(
-            collective_id=0, has_side_effects=True, vmem_limit_bytes=40 * 2**20
+            collective_id=0, has_side_effects=True, vmem_limit_bytes=60 * 2**20
         ),
     )(features, cotangent, sage_weight, attn_weight, tile_vals, tile_dst, tile_src, tile_count, hub_ids, hub_weight)
 

time: 77.6 us -> 66.9 us (0.86)
  Pallas kernels: 68.3 us -> 62.2 us
  local copies, waits for them, and re-layouts: 7.7 us -> 3.19 us
    pallas_call x1, Pallas kernels: 68.3 us -> 62.2 us  [local(): pl.pallas_call(kernel, out_shape=(jax.ShapeDtypeStruct((64, 16, F), BF),...]
    unnamed x21 -> x7, local copies, waits for them, and re-layouts: 7.7 us -> 3.19 us
where the time goes in v2:
time: 66.9 us; the launch traced here: 66.7 us
  Pallas kernels  62.2 us (93%)
  local copies, waits for them, and re-layouts  3.19 us (5%)
  between operations  1.31 us (2%)
    pallas_call x1, Pallas kernels, local(): pl.pallas_call(kernel, out_shape=(jax.ShapeDtypeStruct((64, 16, F), BF),...  62.2 us
    unnamed x7, local copies, waits for them, and re-layouts  3.19 us

profile of v2, /device:TPU:16, one launch (start us, length us, event | category | flops | bytes accessed | tf_op | source)
XLA Modules:
  0.0 66.7 jit_solution(658216141864422425)
XLA Ops:
  1.3 62.2 %shard_map.121 = (bf16[64,16,128]{2,1,0:T(8,128)(2,1)}, bf16[2,512,128]{2,1,0:T(8,128)(2,1)}, f32[1,6,128,128]{3,2,1,0:T(8,128)}) custom-call(bf16[2,512,128]{2,1,0:T(8,128)(2,1)} %feat_h.1, bf16[64,16,128]{2,1,0:T(8,128)(2,1)} %cot_h.1, bf16[2,128,128]{2,1,0:T(8,128)(2,1)} %sw_h.1, bf16[4,128,128]{2,1,0:T(8,128)(2,1)} %aw_h.1, ...), custom_call_target="tpu_custom_call" | custom-call | tf_op jit(solution)/shard_map/pallas_call | solution.py:414
  63.5 0.0 copy-start.1
  63.5 0.0 copy-start
  63.5 1.7 %copy.17 = bf16[64,16,128]{2,1,0:T(8,128)(2,1)} copy(bf16[64,16,128]{2,1,0:T(8,128)(2,1)} %get-tuple-element.6) | data formatting | bytes 524288
  65.2 0.0 copy-done.1
  65.3 0.7 %copy.18 = bf16[2,512,128]{2,1,0:T(8,128)(2,1)} copy(bf16[2,512,128]{2,1,0:T(8,128)(2,1)S(1)} %copy-done.1) | data formatting | bytes 524288
  66.0 0.0 copy-done
  66.0 0.7 %copy.19 = f32[1,6,128,128]{3,2,1,0:T(8,128)} copy(f32[1,6,128,128]{3,2,1,0:T(8,128)S(1)} %copy-done) | data formatting | bytes 786432
Async XLA Ops:
  63.5 1.8 %copy-start.1 = (bf16[2,512,128]{2,1,0:T(8,128)(2,1)S(1)}, bf16[2,512,128]{2,1,0:T(8,128)(2,1)}, u32[]{:S(2)}) copy-start(bf16[2,512,128]{2,1,0:T(8,128)(2,1)} %get-tuple-element.7) | copy-start | bytes 786436
  63.5 2.5 %copy-start = (f32[1,6,128,128]{3,2,1,0:T(8,128)S(1)}, f32[1,6,128,128]{3,2,1,0:T(8,128)}, u32[]{:S(2)}) copy-start(f32[1,6,128,128]{3,2,1,0:T(8,128)} %get-tuple-element.8) | copy-start | bytes 1179652

commit v3 on v2

--- a/solution.py
+++ b/solution.py
@@ -29,10 +29,10 @@
 
 
 def kernel(
-    feat_h, cot_h, sw_h, aw_h, tiles_h, dst, src, cnt, ids, hubw_h,
-    lo_h, gf_h, gw_h,
-    feat, cot, sw, aw, tiles, hubw, lo_out, gf_out, gw_out,
-    adj, adj_t, hub_t, fa_t, acc32, dsil, agg, hid, hall, h32, c32, g32, o32,
+    feat_h, cot_h, sw_h, aw_h, tiles_h, dst_h, src_h, cnt_h, ids_h, hubw_h,
+    lo_h, gf_h, ga_h, gs_h,
+    feat, cot, sw, aw, tiles, hubw, dst, src, cnt, ids, lo_out, gf_out,
+    adj, adj_t, hub_t, fa_t, acc32, dsil, agg, hsend, hall, h32, c32, g32, o32,
     dqkv, hn, mixn, cotn, gmn, gsend, gback, gpre, gacat, tot32,
     hubloc, hub_all, hg_src, hg_buf, ars_src, ars_buf, aag_src, aag_buf,
     srs_src, srs_buf, sag_src, sag_buf,
@@ -46,7 +46,10 @@
     loads = [
         pltpu.make_async_copy(a, b, in_sem.at[i])
         for i, (a, b) in enumerate(
-            ((feat_h, feat), (tiles_h, tiles), (hubw_h, hubw), (sw_h, sw), (cot_h, cot), (aw_h, aw))
+            (
+                (feat_h, feat), (ids_h, ids), (tiles_h, tiles), (dst_h, dst), (src_h, src),
+                (cnt_h, cnt), (hubw_h, hubw), (sw_h, sw), (cot_h, cot), (aw_h, aw),
+            )
         )
     ]
     for load in loads:
@@ -61,8 +64,12 @@
         pl.semaphore_signal(barrier, inc=1, device_id={"graph": lax.rem(g + k, n_g)}, device_id_type=MESH)
         return carry
 
+    def over_config(one):
+        lax.fori_loop(12, n_c, one, 0)
+        lax.fori_loop(1, 12, one, 0)
+
+    over_config(hello_config)
     lax.fori_loop(1, n_g, hello_graph, 0)
-    lax.fori_loop(1, n_c, hello_config, 0)
 
     def send(src_ref, dst_ref, send_sem, recv_sem, where):
         pltpu.make_async_remote_copy(
@@ -76,6 +83,8 @@
     def wait_bytes(ref, sem):
         pltpu.make_async_copy(ref, ref, sem).wait()
 
+    loads[0].wait()
+    loads[1].wait()
     base = g * 512
     row = lax.broadcasted_iota(jnp.int32, (16, 512), 0)
     col = lax.broadcasted_iota(jnp.int32, (16, 512), 1)
@@ -83,7 +92,6 @@
     for j in range(8):
         want = jnp.where(row == j, ids[j] - base, want)
     onehot = jnp.where(col == want, 1.0, 0.0).astype(BF)
-    loads[0].wait()
     x_cat = jnp.concatenate([feat[0], feat[1]], axis=1)
     rows_hub = mm(onehot, x_cat)
     hubloc[...] = jnp.concatenate([rows_hub[:8, :F], rows_hub[:8, F:]], axis=0).astype(BF)
@@ -98,21 +106,32 @@
 
     lax.fori_loop(1, n_g, send_hub, 0)
 
-    for load in loads[1:]:
+    for load in loads[2:]:
         load.wait()
 
-    def build(b, carry):
-        at = pl.multiple_of(b * 128, 128)
+    def halves(block):
+        groups = block.shape[0] // 16
+        split = block.reshape(groups, 2, 8, block.shape[1])
+        return [split[:, h].reshape(groups * 8, block.shape[1]) for h in range(2)]
+
+    def build(pair, carry):
         for s in range(4):
-            acc = jnp.zeros((128, 128), F32)
-            for t in range(12):
-                live = (dst[t] == b) & (src[t] == s) & (t < cnt[0])
-                acc = acc + jnp.where(live, 1.0, 0.0) * tiles[t].astype(F32)
-            adj[pl.ds(at, 128), s * 128 : (s + 1) * 128] = acc.astype(BF)
-            adj_t[s * 128 : (s + 1) * 128, pl.ds(at, 128)] = acc.T.astype(BF)
-        return carry
-
-    lax.fori_loop(0, 4, build, 0)
+            found = []
+            for b_in in range(2):
+                b = pair * 2 + b_in
+                acc = jnp.zeros((128, 128), F32)
+                for t in range(12):
+                    live = (dst[t] == b) & (src[t] == s) & (t < cnt[0])
+                    acc = acc + jnp.where(live, 1.0, 0.0) * tiles[t].astype(F32)
+                adj[pl.ds(pl.multiple_of(b * 128, 128), 128), s * 128 : (s + 1) * 128] = acc.astype(BF)
+                found.append(acc)
+            split = halves(jnp.concatenate(found, axis=0))
+            for h in range(2):
+                columns = pl.ds(pl.multiple_of(h * 256 + pair * 128, 128), 128)
+                adj_t[s * 128 : (s + 1) * 128, columns] = split[h].T.astype(BF)
+        return carry
+
+    lax.fori_loop(0, 2, build, 0)
 
     def first(b, carry):
         rows = pl.ds(pl.multiple_of(b * 128, 128), 128)
@@ -128,29 +147,39 @@
     )
     w_sage = sw[...].reshape(2 * F, F)
 
+    def to_half(h):
+        def one(k, carry):
+            p = lax.rem(c + k, n_c)
+            send(hsend.at[h, p], hall.at[h, c], fwd_s.at[h], fwd_r.at[h], {"config": p})
+            return carry
+
+        return one
+
     def forward(i, carry):
-        b = lax.rem(c // 8 + i, 4)
+        b = lax.rem(c // 8 + 2 + i, 4)
         rows = pl.ds(pl.multiple_of(b * 128, 128), 128)
         acc = acc32[rows, :] + mm(hubw[rows, :], hub_cat)
+        hidden, slope = [], []
         for l in range(2):
             a_l = acc[:, l * F : (l + 1) * F].astype(BF)
             agg[l, rows, :] = a_l
             pre = mm(jnp.concatenate([feat[l, rows, :], a_l], axis=1), w_sage)
             sig = 1.0 / (1.0 + jnp.exp(-pre))
-            dsil[l, rows, :] = sig * (1.0 + pre * (1.0 - sig))
-            hid[l, rows, :] = (pre * sig).astype(BF)
+            slope.append(halves(sig * (1.0 + pre * (1.0 - sig))))
+            hidden.append(halves(pre * sig))
+        for h in range(2):
+            for l in range(2):
+                dsil[pl.ds(pl.multiple_of((h * 2 + l) * 256 + b * 64, 64), 64), :] = slope[l][h]
+            hsend[h, pl.ds(b * 8, 8)] = jnp.concatenate(
+                [hidden[0][h].reshape(8, 8, F), hidden[1][h].reshape(8, 8, F)], axis=1
+            ).astype(BF)
 
         def send_hidden(k, inner):
             p = b * 8 + lax.rem(c + k, 8)
-            piece = hid.at[:, pl.ds(pl.multiple_of(p * 16, 16), 16), :]
 
             @pl.when(p != c)
             def _():
-                send(piece, hall.at[pl.ds(c * 2, 2)], fwd_s, fwd_r, {"config": p})
-
-            @pl.when(p == c)
-            def _():
-                keep(piece, hall.at[pl.ds(c * 2, 2)], fwd_r)
+                send(hsend.at[0, p], hall.at[0, c], fwd_s.at[0], fwd_r.at[0], {"config": p})
 
             return inner
 
@@ -158,6 +187,9 @@
         return carry
 
     lax.fori_loop(0, 4, forward, 0)
+    over_config(to_half(1))
+    for h in range(2):
+        keep(hsend.at[h, c], hall.at[h, c], fwd_r.at[h])
 
     c32[...] = cot[...].astype(F32).reshape(1024, F)
 
@@ -172,13 +204,16 @@
 
     lax.fori_loop(0, 4, cot_nodes, 0)
 
-    hub_t[...] = hubw[...].astype(F32).T.astype(BF)
+    split_hub = halves(hubw[...].astype(F32))
+    for h in range(2):
+        hub_t[:, h * 256 : (h + 1) * 256] = split_hub[h].T.astype(BF)
     for l in range(2):
-        fa_t[0:F, l * 512 : (l + 1) * 512] = feat[l].astype(F32).T.astype(BF)
-        fa_t[F : 2 * F, l * 512 : (l + 1) * 512] = agg[l].astype(F32).T.astype(BF)
-
-    wait_bytes(hall, fwd_r)
-    h32[...] = hall[...].astype(F32).reshape(1024, F)
+        split_feat = halves(feat[l].astype(F32))
+        split_agg = halves(agg[l].astype(F32))
+        for h in range(2):
+            columns = slice((h * 2 + l) * 256, (h * 2 + l + 1) * 256)
+            fa_t[0:F, columns] = split_feat[h].T.astype(BF)
+            fa_t[F : 2 * F, columns] = split_agg[h].T.astype(BF)
 
     w_qkv = jnp.concatenate([aw[0], aw[1], aw[2]], axis=1)
 
@@ -202,7 +237,8 @@
 
     def attend(i, carry):
         rows = pl.ds(pl.multiple_of(i * 256, 256), 256)
-        h_four = jnp.concatenate([h32[pl.ds(i * 4 + k, 64, stride=16), :] for k in range(4)], axis=0)
+        start = (i // 2) * 512 + lax.rem(i, 2) * 4
+        h_four = jnp.concatenate([h32[pl.ds(start + k, 64, stride=8), :] for k in range(4)], axis=0)
         h_b = h_four.astype(BF)
         hn[rows, :] = h_b
         qkv = mm(h_b, w_qkv).astype(BF)
@@ -248,23 +284,26 @@
         back = cotn[rows, :].astype(F32) + mm_nt(grads, w_qkv)
         for k in range(4):
             o32[pl.ds(i * 4 + k, 64, stride=16), :] = out[k * 64 : (k + 1) * 64]
-            g32[pl.ds(i * 4 + k, 64, stride=16), :] = back[k * 64 : (k + 1) * 64]
-        return carry
-
-    lax.fori_loop(0, 4, attend, 0)
-    gsend[...] = g32[...].reshape(64, 16, F).astype(BF)
-
-    def send_back(k, carry):
-        p = lax.rem(c + k, n_c)
-        send(
-            gsend.at[pl.ds(p * 2, 2)],
-            gback.at[:, pl.ds(pl.multiple_of(c * 16, 16), 16), :],
-            back_s, back_r, {"config": p},
-        )
-        return carry
-
-    keep(gsend.at[pl.ds(c * 2, 2)], gback.at[:, pl.ds(pl.multiple_of(c * 16, 16), 16), :], back_r)
-    lax.fori_loop(1, n_c, send_back, 0)
+            g32[pl.ds(start + k, 64, stride=8), :] = back[k * 64 : (k + 1) * 64]
+        return carry
+
+    def half_of_nodes(h, carry):
+        rows = pl.ds(pl.multiple_of(h * 512, 512), 512)
+        wait_bytes(hall.at[h], fwd_r.at[h])
+        h32[rows, :] = hall[h].astype(F32).reshape(512, F)
+        lax.fori_loop(h * 2, h * 2 + 2, attend, 0)
+        gsend[h] = g32[rows, :].reshape(32, 16, F).astype(BF)
+
+        def send_back(k, inner):
+            p = lax.rem(c + k, n_c)
+            send(gsend.at[h, p], gback.at[h, c], back_s.at[h], back_r.at[h], {"config": p})
+            return inner
+
+        over_config(send_back)
+        keep(gsend.at[h, c], gback.at[h, c], back_r.at[h])
+        return carry
+
+    lax.fori_loop(0, 2, half_of_nodes, 0)
 
     lo_out[...] = o32[...].reshape(64, 16, F).astype(BF)
     store_lo = pltpu.make_async_copy(lo_out, lo_h, out_sem.at[0])
@@ -283,21 +322,28 @@
     keep(ars_src.at[c], ars_buf.at[c], ars_r)
     lax.fori_loop(1, n_c, send_attn, 0)
 
-    wait_bytes(gback, back_r)
-
-    def backward(b, carry):
-        rows = pl.ds(pl.multiple_of(b * 128, 128), 128)
+    def slopes(h):
+        wait_bytes(gback.at[h], back_r.at[h])
+        arrived = gback[h].astype(F32).reshape(32, 2, 8, F)
+        parts = []
         for l in range(2):
-            gp = (gback[l, rows, :].astype(F32) * dsil[l, rows, :]).astype(BF)
-            gpre[pl.ds(pl.multiple_of(l * 512 + b * 128, 128), 128), :] = gp
-            both = mm_nt(gp, w_sage)
-            tot32[rows, l * F : (l + 1) * F] = both[:, :F]
-            gacat[rows, l * F : (l + 1) * F] = both[:, F:].astype(BF)
-        return carry
-
-    lax.fori_loop(0, 4, backward, 0)
-
-    srs_src[...] = mm(fa_t[...], gpre[...]).reshape(16, 16, F).astype(BF)
+            rows = slice((h * 2 + l) * 256, (h * 2 + l + 1) * 256)
+            parts.append((arrived[:, l].reshape(256, F) * dsil[rows, :]).astype(BF))
+            gpre[rows, :] = parts[l]
+        return parts
+
+    def through_weights(h, parts):
+        for l in range(2):
+            both = mm_nt(parts[l], w_sage)
+            tot32[:, h, :, l * F : (l + 1) * F] = both[:, :F].reshape(32, 8, F)
+            gacat[h * 256 : (h + 1) * 256, l * F : (l + 1) * F] = both[:, F:].astype(BF)
+
+    parts = slopes(0)
+    through_weights(0, parts)
+    sage_first = mm(fa_t[:, 0:512], gpre[0:512, :])
+    hub_first = mm(hub_t[:, 0:256], gacat[0:256, :])
+    parts = slopes(1)
+    srs_src[...] = (sage_first + mm(fa_t[:, 512:1024], gpre[512:1024, :])).reshape(16, 16, F).astype(BF)
 
     def send_sage(k, carry):
         q = lax.rem(c // 2 + k, 16)
@@ -315,7 +361,8 @@
 
     lax.fori_loop(0, 16, send_sage, 0)
 
-    hub_part = mm(hub_t[...], gacat[...])
+    through_weights(1, parts)
+    hub_part = hub_first + mm(hub_t[:, 256:512], gacat[256:512, :])
     hg_src[...] = jnp.concatenate(
         [hub_part[:, :F].reshape(16, 8, F), hub_part[:, F:].reshape(16, 8, F)], axis=1
     ).astype(BF)
@@ -352,7 +399,8 @@
 
     def back_rows(b, carry):
         rows = pl.ds(pl.multiple_of(b * 128, 128), 128)
-        tot32[rows, :] = tot32[rows, :] + mm(adj_t[rows, :], gacat[...])
+        nodes = pl.ds(b * 8, 8)
+        tot32[nodes] = tot32[nodes] + mm(adj_t[rows, :], gacat[...]).reshape(8, 2, 8, 256)
         return carry
 
     lax.fori_loop(0, 4, back_rows, 0)
@@ -369,26 +417,23 @@
     hub_both = jnp.concatenate([hub_sum[0:8], hub_sum[8:16]], axis=1)
     high = hub_both.astype(BF).astype(F32)
     hub_mat = jnp.concatenate([high, hub_both - high, jnp.zeros((112, 256), F32)], axis=0).astype(BF)
-    total = (tot32[...] + mm(onehot_t, hub_mat)).astype(BF)
+    total = (tot32[...].reshape(512, 256) + mm(onehot_t, hub_mat)).astype(BF)
     gf_out[0] = total[:, :F]
     gf_out[1] = total[:, F:]
     store_gf = pltpu.make_async_copy(gf_out, gf_h, out_sem.at[1])
     store_gf.start()
 
-    scale = 1.0 / math.sqrt(64 * 512)
     wait_bytes(aag_buf, aag_r)
-    for i in range(4):
-        gw_out[0, 2 + i] = aag_buf[i * 8 : (i + 1) * 8].astype(F32).reshape(F, F) * scale
+    store_ga = pltpu.make_async_copy(aag_buf, ga_h, out_sem.at[2])
+    store_ga.start()
     wait_bytes(sag_buf, sag_r)
-    for i in range(2):
-        gw_out[0, i] = sag_buf[i * 8 : (i + 1) * 8].astype(F32).reshape(F, F) * scale
-
-    store_gw = pltpu.make_async_copy(gw_out, gw_h, out_sem.at[2])
-    store_gw.start()
+    store_gs = pltpu.make_async_copy(sag_buf, gs_h, out_sem.at[3])
+    store_gs.start()
 
     wait_bytes(hub_all.at[pl.ds(0, 15)], hub_s)
-    wait_bytes(hall.at[pl.ds(0, 62)], fwd_s)
-    wait_bytes(gsend.at[pl.ds(0, 62)], back_s)
+    for h in range(2):
+        wait_bytes(hall.at[h, pl.ds(0, 31)], fwd_s.at[h])
+        wait_bytes(gback.at[h, pl.ds(0, 31)], back_s.at[h])
     wait_bytes(ars_buf.at[pl.ds(0, 31)], ars_s)
     wait_bytes(hg_buf.at[pl.ds(0, 15)], hg_s)
     wait_bytes(aag_buf.at[pl.ds(0, 31)], aag_s)
@@ -404,22 +449,49 @@
 
     store_lo.wait()
     store_gf.wait()
-    store_gw.wait()
+    store_ga.wait()
+    store_gs.wait()
+
+
+def finish(lo_h, gf_h, ga_h, gs_h, lo_out, gf_out, gw_out, lo, gf, ga, gs, gw, in_sem, out_sem):
+    loads = [
+        pltpu.make_async_copy(a, b, in_sem.at[i])
+        for i, (a, b) in enumerate(((lo_h, lo), (gf_h, gf), (ga_h, ga), (gs_h, gs)))
+    ]
+    stores = [
+        pltpu.make_async_copy(a, b, out_sem.at[i])
+        for i, (a, b) in enumerate(((lo, lo_out), (gf, gf_out), (gw, gw_out)))
+    ]
+    for load in loads:
+        load.start()
+    scale = 1.0 / math.sqrt(64 * 512)
+    loads[2].wait()
+    for i in range(4):
+        gw[0, 2 + i] = ga[i * 8 : (i + 1) * 8].astype(F32).reshape(F, F) * scale
+    loads[3].wait()
+    for i in range(2):
+        gw[0, i] = gs[i * 8 : (i + 1) * 8].astype(F32).reshape(F, F) * scale
+    stores[2].start()
+    for i in range(2):
+        loads[i].wait()
+        stores[i].start()
+    for store in stores:
+        store.wait()
 
 
 def local(features, cotangent, sage_weight, attn_weight, tile_vals, tile_dst, tile_src, tile_count, hub_ids, hub_weight):
-    smem = pl.BlockSpec(memory_space=pltpu.SMEM)
     hbm = pl.BlockSpec(memory_space=pltpu.HBM)
     v = pltpu.VMEM
-    return pl.pallas_call(
+    made = pl.pallas_call(
         kernel,
         out_shape=(
             jax.ShapeDtypeStruct((64, 16, F), BF),
             jax.ShapeDtypeStruct((2, 512, F), BF),
-            jax.ShapeDtypeStruct((1, 6, F, F), F32),
+            jax.ShapeDtypeStruct((32, 16, F), BF),
+            jax.ShapeDtypeStruct((16, 16, F), BF),
         ),
-        in_specs=[hbm] * 5 + [smem] * 4 + [hbm],
-        out_specs=(hbm, hbm, hbm),
+        in_specs=[hbm] * 10,
+        out_specs=(hbm,) * 4,
         scratch_shapes=[
             v((2, 512, F), BF),
             v((64, 16, F), BF),
@@ -427,18 +499,21 @@
             v((4, F, F), BF),
             v((12, F, F), BF),
             v((512, F), BF),
+            pltpu.SMEM((12,), jnp.int32),
+            pltpu.SMEM((12,), jnp.int32),
+            pltpu.SMEM((1,), jnp.int32),
+            pltpu.SMEM((8,), jnp.int32),
             v((64, 16, F), BF),
             v((2, 512, F), BF),
-            v((1, 6, F, F), F32),
             v((512, 512), BF),
             v((512, 512), BF),
             v((128, 512), BF),
             v((256, 1024), BF),
             v((512, 256), F32),
-            v((2, 512, F), F32),
+            v((1024, F), F32),
             v((2, 512, F), BF),
-            v((2, 512, F), BF),
-            v((64, 16, F), BF),
+            v((2, 32, 16, F), BF),
+            v((2, 32, 16, F), BF),
             v((1024, F), F32),
             v((1024, F), F32),
             v((1024, F), F32),
@@ -448,11 +523,11 @@
             v((1024, F), BF),
             v((1024, F), BF),
             v((1024, F), BF),
-            v((64, 16, F), BF),
-            v((2, 512, F), BF),
+            v((2, 32, 16, F), BF),
+            v((2, 32, 16, F), BF),
             v((1024, F), BF),
             v((512, 256), BF),
-            v((512, 256), F32),
+            v((32, 2, 8, 256), F32),
             v((16, F), BF),
             v((16, 16, F), BF),
             v((16, 16, F), BF),
@@ -466,12 +541,33 @@
             v((16, F), BF),
             v((16, 16, F), BF),
         ]
-        + [pltpu.SemaphoreType.DMA] * 16
-        + [pltpu.SemaphoreType.DMA((6,)), pltpu.SemaphoreType.DMA((3,))],
+        + [pltpu.SemaphoreType.DMA((2,))] * 4
+        + [pltpu.SemaphoreType.DMA] * 12
+        + [pltpu.SemaphoreType.DMA((10,)), pltpu.SemaphoreType.DMA((4,))],
         compiler_params=pltpu.CompilerParams(
             collective_id=0, has_side_effects=True, vmem_limit_bytes=60 * 2**20
         ),
     )(features, cotangent, sage_weight, attn_weight, tile_vals, tile_dst, tile_src, tile_count, hub_ids, hub_weight)
+    return pl.pallas_call(
+        finish,
+        out_shape=(
+            jax.ShapeDtypeStruct((64, 16, F), BF),
+            jax.ShapeDtypeStruct((2, 512, F), BF),
+            jax.ShapeDtypeStruct((1, 6, F, F), F32),
+        ),
+        in_specs=[hbm] * 4,
+        out_specs=(hbm,) * 3,
+        scratch_shapes=[
+            v((64, 16, F), BF),
+            v((2, 512, F), BF),
+            v((32, 16, F), BF),
+            v((16, 16, F), BF),
+            v((1, 6, F, F), F32),
+            pltpu.SemaphoreType.DMA((4,)),
+            pltpu.SemaphoreType.DMA((3,)),
+        ],
+        compiler_params=pltpu.CompilerParams(vmem_limit_bytes=60 * 2**20),
+    )(*made)
 
 
 def solution(mesh):

time: 66.9 us -> 57.3 us (0.86)
  the two profiles are of different devices: /device:TPU:16 before, /device:TPU:2 now
where the time goes in v3:
time: 57.3 us; the launch traced here: 57.1 us
  Pallas kernels  55.8 us (97%)
  between operations  1.29 us (2%)
    pallas_call x1, Pallas kernels, local(): pl.pallas_call(kernel, out_shape=(jax.ShapeDtypeStruct((64, 16, F), BF),...  53.7 us
    pallas_call x1, Pallas kernels, local(): pl.pallas_call(finish, out_shape=(jax.ShapeDtypeStruct((64, 16, F), BF),...  2.08 us

profile of v3, /device:TPU:2, one launch (start us, length us, event | category | flops | bytes accessed | tf_op | source)
XLA Modules:
  0.0 57.1 jit_solution(852875759280887769)
XLA Ops:
  1.3 53.7 %shard_map.121 = (bf16[64,16,128]{2,1,0:T(8,128)(2,1)}, bf16[2,512,128]{2,1,0:T(8,128)(2,1)}, bf16[32,16,128]{2,1,0:T(8,128)(2,1)}, bf16[16,16,128]{2,1,0:T(8,128)(2,1)}) custom-call(bf16[2,512,128]{2,1,0:T(8,128)(2,1)} %feat_h.1, bf16[64,16,128]{2,1,0:T(8,128)(2,1)} %cot_h.1, bf16[2,128,128]{2,1,0:T(8,128)(2,1)} %sw_h.1, bf16[4,128,128]{2,1,0:T(8,128)(2,1)} %aw_h.1, ...), custom_call_target="tpu_custom_call" | custom-call | tf_op jit(solution)/shard_map/pallas_call | solution.py:485
  55.0 2.1 %shard_map.122 = (bf16[64,16,128]{2,1,0:T(8,128)(2,1)}, bf16[2,512,128]{2,1,0:T(8,128)(2,1)}, f32[1,6,128,128]{3,2,1,0:T(8,128)}) custom-call(bf16[64,16,128]{2,1,0:T(8,128)(2,1)} %get-tuple-element.7.lo_h, bf16[2,512,128]{2,1,0:T(8,128)(2,1)} %get-tuple-element.8.gf_h, bf16[32,16,128]{2,1,0:T(8,128)(2,1)} %get-tuple-element.9.ga_h, ...), custom_call_target="tpu_custom_call" | custom-call | tf_op jit(solution)/shard_map/pallas_call | solution.py:551

commit v4 on v3

--- a/solution.py
+++ b/solution.py
@@ -34,8 +34,8 @@
     feat, cot, sw, aw, tiles, hubw, dst, src, cnt, ids, lo_out, gf_out,
     adj, adj_t, hub_t, fa_t, acc32, dsil, agg, hsend, hall, h32, c32, g32, o32,
     dqkv, hn, mixn, cotn, gmn, gsend, gback, gpre, gacat, tot32,
-    hubloc, hub_all, hg_src, hg_buf, ars_src, ars_buf, aag_src, aag_buf,
-    srs_src, srs_buf, sag_src, sag_buf,
+    hubloc, hub_all, hg_src, hg_buf, ars_src, ars_buf, aag_src,
+    srs_src, srs_buf, sag_src,
     fwd_s, fwd_r, back_s, back_r, hub_s, hub_r, hg_s, hg_r,
     ars_s, ars_r, aag_s, aag_r, srs_s, srs_r, sag_s, sag_r, in_sem, out_sem,
 ):
@@ -43,6 +43,22 @@
     c = lax.axis_index("config")
     n_g = lax.axis_size("graph")
     n_c = lax.axis_size("config")
+    barrier = pltpu.get_barrier_semaphore()
+
+    def hello_config(k, carry):
+        pl.semaphore_signal(barrier, inc=1, device_id={"config": lax.rem(c + k, n_c)}, device_id_type=MESH)
+        return carry
+
+    def hello_graph(k, carry):
+        pl.semaphore_signal(barrier, inc=1, device_id={"graph": lax.rem(g + k, n_g)}, device_id_type=MESH)
+        return carry
+
+    def over_config(one):
+        lax.fori_loop(12, n_c, one, 0)
+        lax.fori_loop(1, 12, one, 0)
+
+    over_config(hello_config)
+    lax.fori_loop(1, n_g, hello_graph, 0)
     loads = [
         pltpu.make_async_copy(a, b, in_sem.at[i])
         for i, (a, b) in enumerate(
@@ -54,22 +70,6 @@
     ]
     for load in loads:
         load.start()
-    barrier = pltpu.get_barrier_semaphore()
-
-    def hello_config(k, carry):
-        pl.semaphore_signal(barrier, inc=1, device_id={"config": lax.rem(c + k, n_c)}, device_id_type=MESH)
-        return carry
-
-    def hello_graph(k, carry):
-        pl.semaphore_signal(barrier, inc=1, device_id={"graph": lax.rem(g + k, n_g)}, device_id_type=MESH)
-        return carry
-
-    def over_config(one):
-        lax.fori_loop(12, n_c, one, 0)
-        lax.fori_loop(1, 12, one, 0)
-
-    over_config(hello_config)
-    lax.fori_loop(1, n_g, hello_graph, 0)
 
     def send(src_ref, dst_ref, send_sem, recv_sem, where):
         pltpu.make_async_remote_copy(
@@ -104,7 +104,8 @@
         send(hubloc, hub_all.at[g], hub_s, hub_r, {"graph": lax.rem(g + k, n_g)})
         return carry
 
-    lax.fori_loop(1, n_g, send_hub, 0)
+    lax.fori_loop(6, n_g, send_hub, 0)
+    lax.fori_loop(1, 6, send_hub, 0)
 
     for load in loads[2:]:
         load.wait()
@@ -291,7 +292,7 @@
         rows = pl.ds(pl.multiple_of(h * 512, 512), 512)
         wait_bytes(hall.at[h], fwd_r.at[h])
         h32[rows, :] = hall[h].astype(F32).reshape(512, F)
-        lax.fori_loop(h * 2, h * 2 + 2, attend, 0)
+        lax.fori_loop(0, 2, lambda j, x: attend(h * 2 + j, x), 0, unroll=True)
         gsend[h] = g32[rows, :].reshape(32, 16, F).astype(BF)
 
         def send_back(k, inner):
@@ -319,8 +320,6 @@
         send(ars_src.at[p], ars_buf.at[c], ars_s, ars_r, {"config": p})
         return carry
 
-    keep(ars_src.at[c], ars_buf.at[c], ars_r)
-    lax.fori_loop(1, n_c, send_attn, 0)
 
     def slopes(h):
         wait_bytes(gback.at[h], back_r.at[h])
@@ -342,12 +341,14 @@
     through_weights(0, parts)
     sage_first = mm(fa_t[:, 0:512], gpre[0:512, :])
     hub_first = mm(hub_t[:, 0:256], gacat[0:256, :])
+    keep(ars_src.at[c], ars_buf.at[c], ars_r)
+    lax.fori_loop(1, n_c, send_attn, 0)
     parts = slopes(1)
     srs_src[...] = (sage_first + mm(fa_t[:, 512:1024], gpre[512:1024, :])).reshape(16, 16, F).astype(BF)
 
     def send_sage(k, carry):
         q = lax.rem(c // 2 + k, 16)
-        p = q * 2
+        p = q * 2 + lax.rem(q // 2, 2)
 
         @pl.when(p != c)
         def _():
@@ -377,22 +378,22 @@
 
     wait_bytes(ars_buf, ars_r)
     aag_src[...] = jnp.sum(ars_buf[...].astype(F32), axis=0).astype(BF)
-    keep(aag_src, aag_buf.at[c], aag_r)
+    keep(aag_src, ga_h.at[c], aag_r)
 
     def send_attn_sum(k, carry):
-        send(aag_src, aag_buf.at[c], aag_s, aag_r, {"config": lax.rem(c + k, n_c)})
+        send(aag_src, ga_h.at[c], aag_s, aag_r, {"config": lax.rem(c + k, n_c)})
         return carry
 
     lax.fori_loop(1, n_c, send_attn_sum, 0)
 
-    @pl.when(lax.rem(c, 2) == 0)
+    @pl.when(lax.rem(c, 2) == lax.rem(c // 4, 2))
     def _():
         wait_bytes(srs_buf, srs_r)
         sag_src[...] = jnp.sum(srs_buf[...].astype(F32), axis=0).astype(BF)
-        keep(sag_src, sag_buf.at[c // 2], sag_r)
+        keep(sag_src, gs_h.at[c // 2], sag_r)
 
         def send_sage_sum(k, carry):
-            send(sag_src, sag_buf.at[c // 2], sag_s, sag_r, {"config": lax.rem(c + k, n_c)})
+            send(sag_src, gs_h.at[c // 2], sag_s, sag_r, {"config": lax.rem(c + k, n_c)})
             return carry
 
         lax.fori_loop(1, n_c, send_sage_sum, 0)
@@ -423,12 +424,8 @@
     store_gf = pltpu.make_async_copy(gf_out, gf_h, out_sem.at[1])
     store_gf.start()
 
-    wait_bytes(aag_buf, aag_r)
-    store_ga = pltpu.make_async_copy(aag_buf, ga_h, out_sem.at[2])
-    store_ga.start()
-    wait_bytes(sag_buf, sag_r)
-    store_gs = pltpu.make_async_copy(sag_buf, gs_h, out_sem.at[3])
-    store_gs.start()
+    wait_bytes(ga_h, aag_r)
+    wait_bytes(gs_h, sag_r)
 
     wait_bytes(hub_all.at[pl.ds(0, 15)], hub_s)
     for h in range(2):
@@ -436,21 +433,19 @@
         wait_bytes(gback.at[h, pl.ds(0, 31)], back_s.at[h])
     wait_bytes(ars_buf.at[pl.ds(0, 31)], ars_s)
     wait_bytes(hg_buf.at[pl.ds(0, 15)], hg_s)
-    wait_bytes(aag_buf.at[pl.ds(0, 31)], aag_s)
-
-    @pl.when(lax.rem(c, 2) == 0)
+    wait_bytes(ars_buf.at[pl.ds(0, 31)], aag_s)
+
+    @pl.when(lax.rem(c, 2) == lax.rem(c // 4, 2))
     def _():
         wait_bytes(srs_buf.at[pl.ds(0, 15)], srs_s)
-        wait_bytes(aag_buf.at[pl.ds(0, 31)], sag_s)
-
-    @pl.when(lax.rem(c, 2) == 1)
+        wait_bytes(ars_buf.at[pl.ds(0, 31)], sag_s)
+
+    @pl.when(lax.rem(c, 2) != lax.rem(c // 4, 2))
     def _():
         wait_bytes(srs_buf.at[pl.ds(0, 16)], srs_s)
 
     store_lo.wait()
     store_gf.wait()
-    store_ga.wait()
-    store_gs.wait()
 
 
 def finish(lo_h, gf_h, ga_h, gs_h, lo_out, gf_out, gw_out, lo, gf, ga, gs, gw, in_sem, out_sem):
@@ -535,15 +530,13 @@
             v((32, 16, F), BF),
             v((32, 16, F), BF),
             v((16, F), BF),
-            v((32, 16, F), BF),
             v((16, 16, F), BF),
             v((32, 16, F), BF),
             v((16, F), BF),
-            v((16, 16, F), BF),
         ]
         + [pltpu.SemaphoreType.DMA((2,))] * 4
         + [pltpu.SemaphoreType.DMA] * 12
-        + [pltpu.SemaphoreType.DMA((10,)), pltpu.SemaphoreType.DMA((4,))],
+        + [pltpu.SemaphoreType.DMA((10,)), pltpu.SemaphoreType.DMA((2,))],
         compiler_params=pltpu.CompilerParams(
             collective_id=0, has_side_effects=True, vmem_limit_bytes=60 * 2**20
         ),

time: 57.3 us -> 56 us (0.977)
  the two profiles are of different devices: /device:TPU:2 before, /device:TPU:1 now
where the time goes in v4:
time: 56 us; the launch traced here: 55.9 us
  Pallas kernels  54.6 us (98%)
  between operations  1.29 us (2%)
    pallas_call x1, Pallas kernels, local(): pl.pallas_call(kernel, out_shape=(jax.ShapeDtypeStruct((64, 16, F), BF),...  52.5 us
    pallas_call x1, Pallas kernels, local(): pl.pallas_call(finish, out_shape=(jax.ShapeDtypeStruct((64, 16, F), BF),...  2.08 us

profile of v4, /device:TPU:1, one launch (start us, length us, event | category | flops | bytes accessed | tf_op | source)
XLA Modules:
  0.0 55.9 jit_solution(1568063016489207705)
XLA Ops:
  1.3 52.5 %shard_map.121 = (bf16[64,16,128]{2,1,0:T(8,128)(2,1)}, bf16[2,512,128]{2,1,0:T(8,128)(2,1)}, bf16[32,16,128]{2,1,0:T(8,128)(2,1)}, bf16[16,16,128]{2,1,0:T(8,128)(2,1)}) custom-call(bf16[2,512,128]{2,1,0:T(8,128)(2,1)} %feat_h.1, bf16[64,16,128]{2,1,0:T(8,128)(2,1)} %cot_h.1, bf16[2,128,128]{2,1,0:T(8,128)(2,1)} %sw_h.1, bf16[4,128,128]{2,1,0:T(8,128)(2,1)} %aw_h.1, ...), custom_call_target="tpu_custom_call" | custom-call | tf_op jit(solution)/shard_map/pallas_call | solution.py:480
  53.8 2.1 %shard_map.122 = (bf16[64,16,128]{2,1,0:T(8,128)(2,1)}, bf16[2,512,128]{2,1,0:T(8,128)(2,1)}, f32[1,6,128,128]{3,2,1,0:T(8,128)}) custom-call(bf16[64,16,128]{2,1,0:T(8,128)(2,1)} %get-tuple-element.7.lo_h, bf16[2,512,128]{2,1,0:T(8,128)(2,1)} %get-tuple-element.8.gf_h, bf16[32,16,128]{2,1,0:T(8,128)(2,1)} %get-tuple-element.9.ga_h, ...), custom_call_target="tpu_custom_call" | custom-call | tf_op jit(solution)/shard_map/pallas_call | solution.py:544

commit v5 on v4

--- a/solution.py
+++ b/solution.py
@@ -165,7 +165,7 @@
             a_l = acc[:, l * F : (l + 1) * F].astype(BF)
             agg[l, rows, :] = a_l
             pre = mm(jnp.concatenate([feat[l, rows, :], a_l], axis=1), w_sage)
-            sig = 1.0 / (1.0 + jnp.exp(-pre))
+            sig = 0.5 + 0.5 * jnp.tanh(0.5 * pre)
             slope.append(halves(sig * (1.0 + pre * (1.0 - sig))))
             hidden.append(halves(pre * sig))
         for h in range(2):
@@ -260,8 +260,9 @@
         mix = [both[k][:, :F] * inv[k] for k in four]
         gm = [gmn[pl.ds(pl.multiple_of(i * 256 + k * 64, 64), 64), :].astype(F32) * inv[k] for k in four]
         gm_b = [gm[k].astype(BF) for k in four]
-        less = [(-(gm_b[k].astype(F32) * mix[k])).astype(BF) for k in four]
-        dp = [mm_nt(jnp.concatenate([gm_b[k], less[k]], axis=1), val_x[k]) for k in four]
+        less = jnp.concatenate([(gm_b[k].astype(F32) * mix[k]).astype(BF) for k in four], axis=0)
+        less = mm_nt(less, head_mask)
+        dp = [mm_nt(gm_b[k], val_x[k][:, :F]) - less[k * 64 : (k + 1) * 64] for k in four]
         ds = [(w[k].astype(F32) * dp[k] * ((1.0 - t[k] * t[k]) * root)).astype(BF) for k in four]
         d_q = [mm(ds[k], key_x[k]).astype(BF) for k in four]
         right = [
@@ -342,7 +343,7 @@
     sage_first = mm(fa_t[:, 0:512], gpre[0:512, :])
     hub_first = mm(hub_t[:, 0:256], gacat[0:256, :])
     keep(ars_src.at[c], ars_buf.at[c], ars_r)
-    lax.fori_loop(1, n_c, send_attn, 0)
+    over_config(send_attn)
     parts = slopes(1)
     srs_src[...] = (sage_first + mm(fa_t[:, 512:1024], gpre[512:1024, :])).reshape(16, 16, F).astype(BF)
 
@@ -360,7 +361,8 @@
 
         return carry
 
-    lax.fori_loop(0, 16, send_sage, 0)
+    lax.fori_loop(6, 16, send_sage, 0)
+    lax.fori_loop(0, 6, send_sage, 0)
 
     through_weights(1, parts)
     hub_part = hub_first + mm(hub_t[:, 256:512], gacat[256:512, :])
@@ -374,7 +376,8 @@
         return carry
 
     keep(hg_src.at[g], hg_buf.at[g], hg_r)
-    lax.fori_loop(1, n_g, send_hub_grad, 0)
+    lax.fori_loop(6, n_g, send_hub_grad, 0)
+    lax.fori_loop(1, 6, send_hub_grad, 0)
 
     wait_bytes(ars_buf, ars_r)
     aag_src[...] = jnp.sum(ars_buf[...].astype(F32), axis=0).astype(BF)
@@ -384,7 +387,7 @@
         send(aag_src, ga_h.at[c], aag_s, aag_r, {"config": lax.rem(c + k, n_c)})
         return carry
 
-    lax.fori_loop(1, n_c, send_attn_sum, 0)
+    over_config(send_attn_sum)
 
     @pl.when(lax.rem(c, 2) == lax.rem(c // 4, 2))
     def _():
@@ -396,7 +399,7 @@
             send(sag_src, gs_h.at[c // 2], sag_s, sag_r, {"config": lax.rem(c + k, n_c)})
             return carry
 
-        lax.fori_loop(1, n_c, send_sage_sum, 0)
+        over_config(send_sage_sum)
 
     def back_rows(b, carry):
         rows = pl.ds(pl.multiple_of(b * 128, 128), 128)
@@ -449,27 +452,27 @@
 
 
 def finish(lo_h, gf_h, ga_h, gs_h, lo_out, gf_out, gw_out, lo, gf, ga, gs, gw, in_sem, out_sem):
-    loads = [
-        pltpu.make_async_copy(a, b, in_sem.at[i])
-        for i, (a, b) in enumerate(((lo_h, lo), (gf_h, gf), (ga_h, ga), (gs_h, gs)))
-    ]
-    stores = [
-        pltpu.make_async_copy(a, b, out_sem.at[i])
-        for i, (a, b) in enumerate(((lo, lo_out), (gf, gf_out), (gw, gw_out)))
-    ]
+    loads = [pltpu.make_async_copy(ga_h, ga, in_sem.at[0]), pltpu.make_async_copy(gs_h, gs, in_sem.at[1])]
+    stores = [pltpu.make_async_copy(gw.at[0, i], gw_out.at[0, i], out_sem.at[i]) for i in range(6)]
+    for a_h, a, a_out, size in ((lo_h, lo, lo_out, 16), (gf_h, gf, gf_out, 1)):
+        for i in range(a.shape[0] // size):
+            part = pl.ds(i * size, size)
+            loads.append(pltpu.make_async_copy(a_h.at[part], a.at[part], in_sem.at[len(loads)]))
+            stores.append(pltpu.make_async_copy(a.at[part], a_out.at[part], out_sem.at[len(stores)]))
     for load in loads:
         load.start()
     scale = 1.0 / math.sqrt(64 * 512)
-    loads[2].wait()
+    loads[0].wait()
     for i in range(4):
         gw[0, 2 + i] = ga[i * 8 : (i + 1) * 8].astype(F32).reshape(F, F) * scale
-    loads[3].wait()
+        stores[2 + i].start()
+    loads[1].wait()
     for i in range(2):
         gw[0, i] = gs[i * 8 : (i + 1) * 8].astype(F32).reshape(F, F) * scale
-    stores[2].start()
-    for i in range(2):
-        loads[i].wait()
         stores[i].start()
+    for load, store in zip(loads[2:], stores[6:]):
+        load.wait()
+        store.start()
     for store in stores:
         store.wait()
 
@@ -556,8 +559,8 @@
             v((32, 16, F), BF),
             v((16, 16, F), BF),
             v((1, 6, F, F), F32),
-            pltpu.SemaphoreType.DMA((4,)),
-            pltpu.SemaphoreType.DMA((3,)),
+            pltpu.SemaphoreType.DMA((8,)),
+            pltpu.SemaphoreType.DMA((12,)),
         ],
         compiler_params=pltpu.CompilerParams(vmem_limit_bytes=60 * 2**20),
     )(*made)

time: 56 us -> 55.1 us (0.984)
  Pallas kernels: 54.6 us -> 53.6 us
    pallas_call x1, Pallas kernels: 52.5 us -> 51.6 us  [local(): pl.pallas_call(kernel, out_shape=(jax.ShapeDtypeStruct((64, 16, F), BF),...]
where the time goes in v5:
time: 55.1 us; the launch traced here: 54.9 us
  Pallas kernels  53.6 us (97%)
  between operations  1.29 us (2%)
    pallas_call x1, Pallas kernels, local(): pl.pallas_call(kernel, out_shape=(jax.ShapeDtypeStruct((64, 16, F), BF),...  51.6 us
    pallas_call x1, Pallas kernels, local(): pl.pallas_call(finish, out_shape=(jax.ShapeDtypeStruct((64, 16, F), BF),...  2.03 us

profile of v5, /device:TPU:1, one launch (start us, length us, event | category | flops | bytes accessed | tf_op | source)
XLA Modules:
  0.0 54.9 jit_solution(10276228714831745579)
XLA Ops:
  1.3 51.6 %shard_map.121 = (bf16[64,16,128]{2,1,0:T(8,128)(2,1)}, bf16[2,512,128]{2,1,0:T(8,128)(2,1)}, bf16[32,16,128]{2,1,0:T(8,128)(2,1)}, bf16[16,16,128]{2,1,0:T(8,128)(2,1)}) custom-call(bf16[2,512,128]{2,1,0:T(8,128)(2,1)} %feat_h.1, bf16[64,16,128]{2,1,0:T(8,128)(2,1)} %cot_h.1, bf16[2,128,128]{2,1,0:T(8,128)(2,1)} %sw_h.1, bf16[4,128,128]{2,1,0:T(8,128)(2,1)} %aw_h.1, ...), custom_call_target="tpu_custom_call" | custom-call | tf_op jit(solution)/shard_map/pallas_call | solution.py:483
  52.9 2.0 %shard_map.122 = (bf16[64,16,128]{2,1,0:T(8,128)(2,1)}, bf16[2,512,128]{2,1,0:T(8,128)(2,1)}, f32[1,6,128,128]{3,2,1,0:T(8,128)}) custom-call(bf16[64,16,128]{2,1,0:T(8,128)(2,1)} %get-tuple-element.7.lo_h, bf16[2,512,128]{2,1,0:T(8,128)(2,1)} %get-tuple-element.8.gf_h, bf16[32,16,128]{2,1,0:T(8,128)(2,1)} %get-tuple-element.9.ga_h, ...), custom_call_target="tpu_custom_call" | custom-call | tf_op jit(solution)/shard_map/pallas_call | solution.py:547

commit v6 on v5

--- a/solution.py
+++ b/solution.py
@@ -239,8 +239,7 @@
     def attend(i, carry):
         rows = pl.ds(pl.multiple_of(i * 256, 256), 256)
         start = (i // 2) * 512 + lax.rem(i, 2) * 4
-        h_four = jnp.concatenate([h32[pl.ds(start + k, 64, stride=8), :] for k in range(4)], axis=0)
-        h_b = h_four.astype(BF)
+        h_b = jnp.concatenate([h32[pl.ds(start + k, 64, stride=8), :] for k in range(4)], axis=0).astype(BF)
         hn[rows, :] = h_b
         qkv = mm(h_b, w_qkv).astype(BF)
         four = range(4)
@@ -282,10 +281,8 @@
             axis=1,
         )
         dqkv[rows, :] = grads
-        out = h_four + mm(mix_b, aw[3])
         back = cotn[rows, :].astype(F32) + mm_nt(grads, w_qkv)
         for k in range(4):
-            o32[pl.ds(i * 4 + k, 64, stride=16), :] = out[k * 64 : (k + 1) * 64]
             g32[pl.ds(start + k, 64, stride=8), :] = back[k * 64 : (k + 1) * 64]
         return carry
 
@@ -307,6 +304,14 @@
 
     lax.fori_loop(0, 2, half_of_nodes, 0)
 
+    def outputs(i, carry):
+        rows = pl.ds(pl.multiple_of(i * 256, 256), 256)
+        out = hn[rows, :].astype(F32) + mm(mixn[rows, :], aw[3])
+        for k in range(4):
+            o32[pl.ds(i * 4 + k, 64, stride=16), :] = out[k * 64 : (k + 1) * 64]
+        return carry
+
+    lax.fori_loop(0, 4, outputs, 0)
     lo_out[...] = o32[...].reshape(64, 16, F).astype(BF)
     store_lo = pltpu.make_async_copy(lo_out, lo_h, out_sem.at[0])
     store_lo.start()

time: 55.1 us -> 55.1 us (level)
  no operation moved by 1% of the time
where the time goes in v6:
time: 55.1 us; the launch traced here: 54.9 us
  Pallas kernels  53.6 us (97%)
  between operations  1.29 us (2%)
    pallas_call x1, Pallas kernels, local(): pl.pallas_call(kernel, out_shape=(jax.ShapeDtypeStruct((64, 16, F), BF),...  51.6 us
    pallas_call x1, Pallas kernels, local(): pl.pallas_call(finish, out_shape=(jax.ShapeDtypeStruct((64, 16, F), BF),...  2.03 us

profile of v6, /device:TPU:1, one launch (start us, length us, event | category | flops | bytes accessed | tf_op | source)
XLA Modules:
  0.0 54.9 jit_solution(13576987023484768072)
XLA Ops:
  1.3 51.6 %shard_map.121 = (bf16[64,16,128]{2,1,0:T(8,128)(2,1)}, bf16[2,512,128]{2,1,0:T(8,128)(2,1)}, bf16[32,16,128]{2,1,0:T(8,128)(2,1)}, bf16[16,16,128]{2,1,0:T(8,128)(2,1)}) custom-call(bf16[2,512,128]{2,1,0:T(8,128)(2,1)} %feat_h.1, bf16[64,16,128]{2,1,0:T(8,128)(2,1)} %cot_h.1, bf16[2,128,128]{2,1,0:T(8,128)(2,1)} %sw_h.1, bf16[4,128,128]{2,1,0:T(8,128)(2,1)} %aw_h.1, ...), custom_call_target="tpu_custom_call" | custom-call | tf_op jit(solution)/shard_map/pallas_call | solution.py:488
  52.8 2.0 %shard_map.122 = (bf16[64,16,128]{2,1,0:T(8,128)(2,1)}, bf16[2,512,128]{2,1,0:T(8,128)(2,1)}, f32[1,6,128,128]{3,2,1,0:T(8,128)}) custom-call(bf16[64,16,128]{2,1,0:T(8,128)(2,1)} %get-tuple-element.7.lo_h, bf16[2,512,128]{2,1,0:T(8,128)(2,1)} %get-tuple-element.8.gf_h, bf16[32,16,128]{2,1,0:T(8,128)(2,1)} %get-tuple-element.9.ga_h, ...), custom_call_target="tpu_custom_call" | custom-call | tf_op jit(solution)/shard_map/pallas_call | solution.py:552

commit v7 on v6

--- a/solution.py
+++ b/solution.py
@@ -33,7 +33,7 @@
     lo_h, gf_h, ga_h, gs_h,
     feat, cot, sw, aw, tiles, hubw, dst, src, cnt, ids, lo_out, gf_out,
     adj, adj_t, hub_t, fa_t, acc32, dsil, agg, hsend, hall, h32, c32, g32, o32,
-    dqkv, hn, mixn, cotn, gmn, gsend, gback, gpre, gacat, tot32,
+    dqkv, hn, mixn, cotn, gmn, gsend, gback, gacat, tot32,
     hubloc, hub_all, hg_src, hg_buf, ars_src, ars_buf, aag_src,
     srs_src, srs_buf, sag_src,
     fwd_s, fwd_r, back_s, back_r, hub_s, hub_r, hg_s, hg_r,
@@ -334,7 +334,6 @@
         for l in range(2):
             rows = slice((h * 2 + l) * 256, (h * 2 + l + 1) * 256)
             parts.append((arrived[:, l].reshape(256, F) * dsil[rows, :]).astype(BF))
-            gpre[rows, :] = parts[l]
         return parts
 
     def through_weights(h, parts):
@@ -345,12 +344,13 @@
 
     parts = slopes(0)
     through_weights(0, parts)
-    sage_first = mm(fa_t[:, 0:512], gpre[0:512, :])
+    sage_first = mm(fa_t[:, 0:256], parts[0]) + mm(fa_t[:, 256:512], parts[1])
     hub_first = mm(hub_t[:, 0:256], gacat[0:256, :])
     keep(ars_src.at[c], ars_buf.at[c], ars_r)
     over_config(send_attn)
     parts = slopes(1)
-    srs_src[...] = (sage_first + mm(fa_t[:, 512:1024], gpre[512:1024, :])).reshape(16, 16, F).astype(BF)
+    sage_all = sage_first + mm(fa_t[:, 512:768], parts[0]) + mm(fa_t[:, 768:1024], parts[1])
+    srs_src[...] = sage_all.reshape(16, 16, F).astype(BF)
 
     def send_sage(k, carry):
         q = lax.rem(c // 2 + k, 16)
@@ -528,7 +528,6 @@
             v((1024, F), BF),
             v((2, 32, 16, F), BF),
             v((2, 32, 16, F), BF),
-            v((1024, F), BF),
             v((512, 256), BF),
             v((32, 2, 8, 256), F32),
             v((16, F), BF),

time: 55.1 us -> 55.1 us (level)
  no operation moved by 1% of the time
where the time goes in v7:
time: 55.1 us; the launch traced here: 54.9 us
  Pallas kernels  53.6 us (97%)
  between operations  1.29 us (2%)
    pallas_call x1, Pallas kernels, local(): pl.pallas_call(kernel, out_shape=(jax.ShapeDtypeStruct((64, 16, F), BF),...  51.6 us
    pallas_call x1, Pallas kernels, local(): pl.pallas_call(finish, out_shape=(jax.ShapeDtypeStruct((64, 16, F), BF),...  2.03 us

profile of v7, /device:TPU:1, one launch (start us, length us, event | category | flops | bytes accessed | tf_op | source)
XLA Modules:
  0.0 54.9 jit_solution(16538764676495871768)
XLA Ops:
  1.3 51.6 %shard_map.121 = (bf16[64,16,128]{2,1,0:T(8,128)(2,1)}, bf16[2,512,128]{2,1,0:T(8,128)(2,1)}, bf16[32,16,128]{2,1,0:T(8,128)(2,1)}, bf16[16,16,128]{2,1,0:T(8,128)(2,1)}) custom-call(bf16[2,512,128]{2,1,0:T(8,128)(2,1)} %feat_h.1, bf16[64,16,128]{2,1,0:T(8,128)(2,1)} %cot_h.1, bf16[2,128,128]{2,1,0:T(8,128)(2,1)} %sw_h.1, bf16[4,128,128]{2,1,0:T(8,128)(2,1)} %aw_h.1, ...), custom_call_target="tpu_custom_call" | custom-call | tf_op jit(solution)/shard_map/pallas_call | solution.py:488
  52.9 2.0 %shard_map.122 = (bf16[64,16,128]{2,1,0:T(8,128)(2,1)}, bf16[2,512,128]{2,1,0:T(8,128)(2,1)}, f32[1,6,128,128]{3,2,1,0:T(8,128)}) custom-call(bf16[64,16,128]{2,1,0:T(8,128)(2,1)} %get-tuple-element.7.lo_h, bf16[2,512,128]{2,1,0:T(8,128)(2,1)} %get-tuple-element.8.gf_h, bf16[32,16,128]{2,1,0:T(8,128)(2,1)} %get-tuple-element.9.ga_h, ...), custom_call_target="tpu_custom_call" | custom-call | tf_op jit(solution)/shard_map/pallas_call | solution.py:551
